TPU v7x, 512 devices: a whole 4x8x8 slice. The times are simulated.
512 devices in a mesh: ctx: 64 (over y_hi, z, core), head: 8 (over x, y_lo).
Axes of the slice: x: 4, y: 8 (y_hi: 4, y_lo: 2; y = y_hi * 2 + y_lo), z: 8, core: 2. Of those that a mesh axis runs over, the one named last changes fastest.
Arguments:
- queries: bfloat16 [8192, 6144], P('ctx', 'head'), may hold values from -320 to 320
- latent: bfloat16 [8192, 576], P('ctx'), may hold values from -6 to 6
- w_key: bfloat16 [512, 4096], P(None, 'head'), may hold values from -0.25 to 0.25
- w_value: bfloat16 [512, 4096], P(None, 'head'), may hold values from -0.25 to 0.25
- grad_out: bfloat16 [8192, 4096], P('ctx', 'head'), may hold values from -6 to 6
- segment_ids: int32 [8192], replicated, may hold values from 0 to 31, never falling along the last dimension, each value on 1 to 512 neighbouring positions
Outputs:
- attn_out: bfloat16 [8192, 4096], P('ctx', 'head')
- grad_queries: bfloat16 [8192, 6144], P('ctx', 'head')
- grad_latent: bfloat16 [8192, 576], P('ctx')
- grad_w_key: bfloat16 [512, 4096], P(None, 'head')
- grad_w_value: bfloat16 [512, 4096], P(None, 'head')
Inputs may be any that keep to these rules, and one draw needn't show every extreme that they name: `segment_ids`: document ids never fall along the sequence; each document has at most 512 tokens and one has exactly 512.
All inputs are finite; a program needn't handle non-finite values.
Results may differ from a plain program's by a relative error of at most 0.03.
Values may be sent and summed in bfloat16 or wider, within the bound.
A program may use at most 64 MiB of HBM per device.

v0:
```python
import math

import jax
import jax.numpy as jnp
from jax import lax
from jax.sharding import PartitionSpec as P

LAT = 512
ROPE = 64
NOPE = 128
VDIM = 128
PREV = 4


def from_behind(block, axis, distance):
    devices = range(lax.axis_size(axis))
    route = [(i - distance, i) for i in devices if i - distance in devices]
    return lax.ppermute(block, axis, route)


def as_sent(shard):

    def short(part):
        return part.astype(jnp.bfloat16) if part.dtype == jnp.float32 else part

    return jax.tree.map(short, shard)


def per_device(queries, latent, w_key, w_value, grad_out, segment_ids):
    tok_rows = queries.shape[0]
    head_count = w_key.shape[1] // NOPE
    window = (PREV + 1) * tok_rows
    margin = PREV * tok_rows
    scale_factor = 1.0 / math.sqrt(NOPE + ROPE)
    position = lax.axis_index("ctx")
    latent_nope = latent[:, :LAT]
    own_block = (latent_nope, latent[:, LAT:])
    arrived = [own_block]
    moving = own_block
    for distance in range(PREV):
        moving = from_behind((moving[0], moving[1]), "ctx", 1)
        arrived.append(moving)
    ordered = arrived[::-1]
    first_part = jnp.concatenate([element[0] for element in ordered], 0)
    window_rope = jnp.concatenate([element[1] for element in ordered], 0)
    key_flat = jnp.dot(first_part, w_key, preferred_element_type=jnp.float32).astype(jnp.bfloat16)
    value_flat = jnp.dot(first_part, w_value, preferred_element_type=jnp.float32).astype(
        jnp.bfloat16
    )
    key_nope = key_flat.reshape(window, head_count, NOPE)
    value_block = value_flat.reshape(window, head_count, VDIM)
    row_start = position * tok_rows
    query_pos = row_start + jnp.arange(tok_rows, dtype=jnp.int32)
    key_pos = row_start - margin + jnp.arange(window, dtype=jnp.int32)
    segment_padded = jnp.concatenate([jnp.full((margin,), -1, jnp.int32), segment_ids], 0)
    query_segment = lax.dynamic_slice_in_dim(segment_ids, row_start, tok_rows, 0)
    key_segment = lax.dynamic_slice_in_dim(segment_padded, row_start, window, 0)
    allowed = (
        (key_pos[None, :] <= query_pos[:, None])
        & (key_pos[None, :] >= 0)
        & (key_segment[None, :] == query_segment[:, None])
    )
    query_all = queries.reshape(tok_rows, head_count, NOPE + ROPE)
    query_nope = query_all[:, :, :NOPE]
    query_rope = query_all[:, :, NOPE:]
    upstream = grad_out.reshape(tok_rows, head_count, VDIM)
    scores = scale_factor * (
        jnp.einsum("thd,whd->htw", query_nope, key_nope, preferred_element_type=jnp.float32)
        + jnp.einsum("thd,wd->htw", query_rope, window_rope, preferred_element_type=jnp.float32)
    )
    masked = jnp.where(allowed[None], scores, -jnp.inf)
    row_max = jnp.max(masked, axis=2, keepdims=True)
    exponent = jnp.where(allowed[None], jnp.exp(masked - row_max), 0.0)
    row_total = jnp.sum(exponent, axis=2, keepdims=True)
    weights = exponent.astype(jnp.bfloat16)
    mixed_out = (
        jnp.einsum("htw,whd->htd", weights, value_block, preferred_element_type=jnp.float32)
        / row_total
    )
    attn_block = mixed_out.transpose(1, 0, 2).astype(jnp.bfloat16)
    probability = exponent / row_total
    delta_rows = jnp.sum(upstream.astype(jnp.float32) * attn_block.astype(jnp.float32), axis=2).T[
        :, :, None
    ]
    grad_probs = jnp.einsum(
        "thd,whd->htw", upstream, value_block, preferred_element_type=jnp.float32
    )
    grad_scores = (probability * (grad_probs - delta_rows)).astype(jnp.bfloat16)
    grad_query = scale_factor * jnp.concatenate(
        [
            jnp.einsum("htw,whd->thd", grad_scores, key_nope, preferred_element_type=jnp.float32),
            jnp.einsum("htw,wd->thd", grad_scores, window_rope, preferred_element_type=jnp.float32),
        ],
        2,
    )
    term_nope = (
        scale_factor
        * jnp.einsum("htw,thd->whd", grad_scores, query_nope, preferred_element_type=jnp.float32)
    ).astype(jnp.bfloat16)
    term_rope = (
        scale_factor
        * jnp.einsum("htw,thd->whd", grad_scores, query_rope, preferred_element_type=jnp.float32)
    ).astype(jnp.bfloat16)
    term_value = jnp.einsum(
        "htw,thd->whd",
        probability.astype(jnp.bfloat16),
        upstream,
        preferred_element_type=jnp.float32,
    ).astype(jnp.bfloat16)
    rope_term = jnp.sum(term_rope.astype(jnp.float32), axis=1)
    nope_flat = term_nope.reshape(window, head_count * NOPE)
    value_flat_grad = term_value.reshape(window, head_count * VDIM)
    first_term = jnp.dot(nope_flat, w_key.T, preferred_element_type=jnp.float32) + jnp.dot(
        value_flat_grad, w_value.T, preferred_element_type=jnp.float32
    )
    weight_key = jnp.dot(first_part.T, nope_flat, preferred_element_type=jnp.float32)
    weight_value = jnp.dot(first_part.T, value_flat_grad, preferred_element_type=jnp.float32)
    pieces = [
        (
            first_term[offset * tok_rows : (offset + 1) * tok_rows],
            rope_term[offset * tok_rows : (offset + 1) * tok_rows],
        )
        for offset in range(PREV + 1)
    ]
    gathered_sum = pieces[0]
    for distance in range(PREV):
        incoming = jax.tree.map(
            lambda part, own: part.astype(own.dtype),
            from_behind(as_sent(gathered_sum), "ctx", -1),
            gathered_sum,
        )
        gathered_sum = (
            incoming[0] + pieces[distance + 1][0],
            incoming[1] + pieces[distance + 1][1],
        )
    nope_grad = gathered_sum[0]
    nope_total, rope_total = lax.psum((nope_grad, gathered_sum[1]), "head")
    weight_key, weight_value = lax.psum((weight_key, weight_value), "ctx")
    grad_latent = jnp.concatenate([nope_total, rope_total], 1).astype(jnp.bfloat16)
    attn_out = attn_block.reshape(tok_rows, head_count * VDIM)
    grad_queries = grad_query.astype(jnp.bfloat16).reshape(tok_rows, head_count * (NOPE + ROPE))
    return (
        attn_out,
        grad_queries,
        grad_latent,
        weight_key.astype(jnp.bfloat16),
        weight_value.astype(jnp.bfloat16),
    )


def solution(mesh):
    return jax.shard_map(
        per_device,
        mesh=mesh,
        in_specs=(
            P("ctx", "head"),
            P("ctx", None),
            P(None, "head"),
            P(None, "head"),
            P("ctx", "head"),
            P(),
        ),
        out_specs=(
            P("ctx", "head"),
            P("ctx", "head"),
            P("ctx", None),
            P(None, "head"),
            P(None, "head"),
        ),
        check_vma=False,
    )
```

profile of v0, /device:TPU:32, one launch (start us, length us, event | category | flops | bytes accessed | tf_op | source)
XLA Modules:
  0.0 470.9 jit_solution(15352131798243041736)
XLA Ops:
  0.6 0.0 copy-start
  0.6 0.0 copy-start.4
  0.7 1.0 slice.44
  1.6 1.9 collective-permute-start
  3.6 0.7 slice.46
  4.3 4.4 collective-permute-start.4
  8.7 0.8 pad_dynamic-slice_fusion
  9.5 6.7 %collective-permute-done.4 = bf16[128,64]{0,1:T(8,128)(2,1)S(1)} collective-permute-done((bf16[128,64]{0,1:T(8,128)(2,1)S(1)}, bf16[128,64]{0,1:T(8,128)(2,1)S(1)}, u32[]{:S(2)}, u32[]{:S(2)}) %collective-permute-start.4) | collective-permute-done | bytes 16416 | tf_op jit(solution)/shard_map/ppermute | solution.py:18
  16.2 1.9 collective-permute-start.5
  18.1 7.3 %collective-permute-done.5 = bf16[128,64]{0,1:T(8,128)(2,1)S(1)} collective-permute-done((bf16[128,64]{0,1:T(8,128)(2,1)S(1)}, bf16[128,64]{0,1:T(8,128)(2,1)S(1)}, u32[]{:S(2)}, u32[]{:S(2)}) %collective-permute-start.5) | collective-permute-done | bytes 16416 | tf_op jit(solution)/shard_map/ppermute | solution.py:18
  25.5 1.9 collective-permute-start.6
  27.4 0.8 dynamic_slice.7
  28.2 6.6 %collective-permute-done.6 = bf16[128,64]{0,1:T(8,128)(2,1)S(1)} collective-permute-done((bf16[128,64]{0,1:T(8,128)(2,1)S(1)}, bf16[128,64]{0,1:T(8,128)(2,1)S(1)}, u32[]{:S(2)}, u32[]{:S(2)}) %collective-permute-start.6) | collective-permute-done | bytes 16416 | tf_op jit(solution)/shard_map/ppermute | solution.py:18
  34.7 1.9 collective-permute-start.7
  36.7 0.3 compare_and_fusion
  37.0 1.0 copy.68
  38.0 0.0 copy-start.7
  38.0 1.1 copy.64
  39.2 0.0 collective-permute-done
  39.2 1.9 collective-permute-start.1
  41.1 2.9 collective-permute-done.7
  44.0 5.8 %collective-permute-done.1 = bf16[128,512]{0,1:T(8,128)(2,1)S(1)} collective-permute-done((bf16[128,512]{0,1:T(8,128)(2,1)S(1)}, bf16[128,512]{0,1:T(8,128)(2,1)S(1)}, u32[]{:S(2)}, u32[]{:S(2)}) %collective-permute-start.1) | collective-permute-done | bytes 131104 | tf_op jit(solution)/shard_map/ppermute | solution.py:18
  49.8 1.9 collective-permute-start.2
  51.7 8.6 %collective-permute-done.2 = bf16[128,512]{0,1:T(8,128)(2,1)S(1)} collective-permute-done((bf16[128,512]{0,1:T(8,128)(2,1)S(1)}, bf16[128,512]{0,1:T(8,128)(2,1)S(1)}, u32[]{:S(2)}, u32[]{:S(2)}) %collective-permute-start.2) | collective-permute-done | bytes 131104 | tf_op jit(solution)/shard_map/ppermute | solution.py:18
  60.3 1.9 collective-permute-start.3
  62.2 0.7 constant_dynamic-update-slice_fusion.5
  62.9 7.8 %collective-permute-done.3 = bf16[128,512]{0,1:T(8,128)(2,1)S(1)} collective-permute-done((bf16[128,512]{0,1:T(8,128)(2,1)S(1)}, bf16[128,512]{0,1:T(8,128)(2,1)S(1)}, u32[]{:S(2)}, u32[]{:S(2)}) %collective-permute-start.3) | collective-permute-done | bytes 131104 | tf_op jit(solution)/shard_map/ppermute | solution.py:18
  71.0 0.6 convolution_convert_fusion.2
  71.6 0.4 convolution_bitcast_fusion.1
  72.0 0.3 fusion.6
  72.4 0.0 copy-start.5
  72.4 1.5 fusion.35
  73.9 1.5 convolution_convert_fusion.1
  75.3 2.3 multiply_reduce_fusion
  77.6 1.9 fusion.9
  79.5 0.2 convolution_bitcast_fusion.4
  79.8 0.3 convolution_bitcast_fusion.3
  80.1 0.4 fusion.13
  80.5 0.4 fusion.10
  80.9 2.4 convolution_convert_fusion
  83.3 0.6 fusion.36
  83.8 0.5 copy-done.2
  84.4 0.6 fusion.37
  85.0 0.0 copy-start.6
  85.0 2.1 collective-permute-start.12
  87.1 1.6 fusion.38
  88.6 0.6 convolution_add_fusion
  89.2 298.6 %all-reduce.6 = (bf16[512,512]{1,0:T(8,128)(2,1)}, bf16[512,512]{1,0:T(8,128)(2,1)}) all-reduce(f32[512,512]{1,0:T(8,128)S(1)} %fusion.37, f32[512,512]{1,0:T(8,128)} %fusion.38), channel_id=1, replica_groups=mesh['ctx'=64,'head'=8] {'ctx'}, use_global_device_ids=true, to_apply=%region_6.7 | all-reduce | flops 524288 | bytes 3145728 | tf_op jit(solution)/shard_map/psum | solution.py:138
  387.9 1.7 copy.78
  389.5 0.8 copy.79
  390.4 2.7 collective-permute-start.8
  393.2 1.9 collective-permute-start.13
  395.1 0.5 collective-permute-done.8
  395.7 8.1 %collective-permute-start.9 = (bf16[128,512]{1,0:T(8,128)(2,1)S(1)}, bf16[128,512]{1,0:T(8,128)(2,1)S(1)}, u32[]{:S(2)}, u32[]{:S(2)}) collective-permute-start(bf16[128,512]{1,0:T(8,128)(2,1)S(1)} %fusion.21), channel_id=1, source_target_pairs={{8,0},{16,8},{24,16},{32,24},{40,32},{48,40},{56,48},{64,56},{72,6... | collective-permute-start | bytes 393224 | tf_op jit(solution)/shard_map/ppermute | solution.py:18
  403.8 1.9 collective-permute-start.14
  405.7 0.5 collective-permute-done.9
  406.3 8.1 %collective-permute-start.10 = (bf16[128,512]{1,0:T(8,128)(2,1)S(1)}, bf16[128,512]{1,0:T(8,128)(2,1)S(1)}, u32[]{:S(2)}, u32[]{:S(2)}) collective-permute-start(bf16[128,512]{1,0:T(8,128)(2,1)S(1)} %fusion.20), channel_id=1, source_target_pairs={{8,0},{16,8},{24,16},{32,24},{40,32},{48,40},{56,48},{64,56},{72,6... | collective-permute-start | bytes 393224 | tf_op jit(solution)/shard_map/ppermute | solution.py:18
  414.4 1.9 collective-permute-start.15
  416.4 0.5 collective-permute-done.10
  416.9 8.0 %collective-permute-start.11 = (bf16[128,512]{1,0:T(8,128)(2,1)S(1)}, bf16[128,512]{1,0:T(8,128)(2,1)S(1)}, u32[]{:S(2)}, u32[]{:S(2)}) collective-permute-start(bf16[128,512]{1,0:T(8,128)(2,1)S(1)} %fusion.19), channel_id=1, source_target_pairs={{8,0},{16,8},{24,16},{32,24},{40,32},{48,40},{56,48},{64,56},{72,6... | collective-permute-start | bytes 393224 | tf_op jit(solution)/shard_map/ppermute | solution.py:18
  425.0 2.5 collective-permute-done.11
  427.5 42.5 %all-reduce.5 = (bf16[128,64]{0,1:T(8,128)(2,1)S(1)}, bf16[128,512]{1,0:T(8,128)(2,1)S(1)}) all-reduce(f32[128,64]{0,1:T(8,128)S(1)} %slice_add_fusion.4, f32[128,512]{1,0:T(8,128)S(1)} %slice_add_fusion), channel_id=1, replica_groups=mesh['ctx'=64,'head'=8] {'head'}, use_global_device_ids=true, to_apply=%region_5.6 | all-reduce | flops 73728 | bytes 442368 | tf_op jit(solution)/shard_map/psum | solution.py:137
  470.0 0.1 copy.77
  470.1 0.8 copy.80
  (37 shorter events, 0.5 us)
Async XLA Ops:
  0.6 70.3 %copy-start = (bf16[512,512]{1,0:T(8,128)(2,1)S(1)}, bf16[512,512]{1,0:T(8,128)(2,1)}, u32[]{:S(2)}) copy-start(bf16[512,512]{1,0:T(8,128)(2,1)} %param.8) | copy-start | bytes 1572868
  0.6 70.3 %copy-start.4 = (bf16[128,576]{0,1:T(8,128)(2,1)S(1)}, bf16[128,576]{0,1:T(8,128)(2,1)}, u32[]{:S(2)}) copy-start(bf16[128,576]{0,1:T(8,128)(2,1)} %param.7) | copy-start | bytes 442372
  1.6 37.5 %collective-permute-start = (bf16[128,512]{0,1:T(8,128)(2,1)S(1)}, bf16[128,512]{0,1:T(8,128)(2,1)S(1)}, u32[]{:S(2)}, u32[]{:S(2)}) collective-permute-start(bf16[128,512]{0,1:T(8,128)(2,1)S(1)} %slice.44), channel_id=1, source_target_pairs={{0,8},{8,16},{16,24},{24,32},{32,40},{40,48},{48,56},{56,64},{64,7... | collective-permute-start | bytes 393224 | tf_op jit(solution)/shard_map/ppermute | solution.py:18
  4.3 11.9 %collective-permute-start.4 = (bf16[128,64]{0,1:T(8,128)(2,1)S(1)}, bf16[128,64]{0,1:T(8,128)(2,1)S(1)}, u32[]{:S(2)}, u32[]{:S(2)}) collective-permute-start(bf16[128,64]{0,1:T(8,128)(2,1)S(1)} %slice.46), channel_id=1, source_target_pairs={{0,8},{8,16},{16,24},{24,32},{32,40},{40,48},{48,56},{56,64},{64,7... | collective-permute-start | bytes 49160 | tf_op jit(solution)/shard_map/ppermute | solution.py:18
  16.2 9.3 %collective-permute-start.5 = (bf16[128,64]{0,1:T(8,128)(2,1)S(1)}, bf16[128,64]{0,1:T(8,128)(2,1)S(1)}, u32[]{:S(2)}, u32[]{:S(2)}) collective-permute-start(bf16[128,64]{0,1:T(8,128)(2,1)S(1)} %collective-permute-done.4), channel_id=1, source_target_pairs={{0,8},{8,16},{16,24},{24,32},{32,40},{40,48},{48,56},{56,64},{64,7... | collective-permute-start | bytes 49160 | tf_op jit(solution)/shard_map/ppermute | solution.py:18
  25.5 9.3 %collective-permute-start.6 = (bf16[128,64]{0,1:T(8,128)(2,1)S(1)}, bf16[128,64]{0,1:T(8,128)(2,1)S(1)}, u32[]{:S(2)}, u32[]{:S(2)}) collective-permute-start(bf16[128,64]{0,1:T(8,128)(2,1)S(1)} %collective-permute-done.5), channel_id=1, source_target_pairs={{0,8},{8,16},{16,24},{24,32},{32,40},{40,48},{48,56},{56,64},{64,7... | collective-permute-start | bytes 49160 | tf_op jit(solution)/shard_map/ppermute | solution.py:18
  34.7 9.3 %collective-permute-start.7 = (bf16[128,64]{0,1:T(8,128)(2,1)S(1)}, bf16[128,64]{0,1:T(8,128)(2,1)S(1)}, u32[]{:S(2)}, u32[]{:S(2)}) collective-permute-start(bf16[128,64]{0,1:T(8,128)(2,1)S(1)} %collective-permute-done.6), channel_id=1, source_target_pairs={{0,8},{8,16},{16,24},{24,32},{32,40},{40,48},{48,56},{56,64},{64,7... | collective-permute-start | bytes 49160 | tf_op jit(solution)/shard_map/ppermute | solution.py:18
  38.0 39.6 %copy-start.7 = (bf16[128,512]{0,1:T(8,128)(2,1)}, bf16[128,512]{0,1:T(8,128)(2,1)S(1)}, u32[]{:S(2)}) copy-start(bf16[128,512]{0,1:T(8,128)(2,1)S(1)} %copy.68) | copy-start | bytes 393220
  39.2 10.6 %collective-permute-start.1 = (bf16[128,512]{0,1:T(8,128)(2,1)S(1)}, bf16[128,512]{0,1:T(8,128)(2,1)S(1)}, u32[]{:S(2)}, u32[]{:S(2)}) collective-permute-start(bf16[128,512]{0,1:T(8,128)(2,1)S(1)} %collective-permute-done), channel_id=1, source_target_pairs={{0,8},{8,16},{16,24},{24,32},{32,40},{40,48},{48,56},{56,64},{64,7... | collective-permute-start | bytes 393224 | tf_op jit(solution)/shard_map/ppermute | solution.py:18
  49.8 10.5 %collective-permute-start.2 = (bf16[128,512]{0,1:T(8,128)(2,1)S(1)}, bf16[128,512]{0,1:T(8,128)(2,1)S(1)}, u32[]{:S(2)}, u32[]{:S(2)}) collective-permute-start(bf16[128,512]{0,1:T(8,128)(2,1)S(1)} %collective-permute-done.1), channel_id=1, source_target_pairs={{0,8},{8,16},{16,24},{24,32},{32,40},{40,48},{48,56},{56,64},{64,7... | collective-permute-start | bytes 393224 | tf_op jit(solution)/shard_map/ppermute | solution.py:18
  60.3 10.5 %collective-permute-start.3 = (bf16[128,512]{0,1:T(8,128)(2,1)S(1)}, bf16[128,512]{0,1:T(8,128)(2,1)S(1)}, u32[]{:S(2)}, u32[]{:S(2)}) collective-permute-start(bf16[128,512]{0,1:T(8,128)(2,1)S(1)} %collective-permute-done.2), channel_id=1, source_target_pairs={{0,8},{8,16},{16,24},{24,32},{32,40},{40,48},{48,56},{56,64},{64,7... | collective-permute-start | bytes 393224 | tf_op jit(solution)/shard_map/ppermute | solution.py:18
  71.0 2.9 copy-start.1
  72.4 1.5 copy-start.5
  83.3 1.1 copy-start.2
  84.4 2.7 copy-start.3
  85.0 3.7 copy-start.6
  85.0 308.1 %collective-permute-start.12 = (bf16[128,64]{0,1:T(8,128)(2,1)S(1)}, bf16[128,64]{0,1:T(8,128)(2,1)S(1)}, u32[]{:S(2)}, u32[]{:S(2)}) collective-permute-start(bf16[128,64]{0,1:T(8,128)(2,1)S(1)} %slice.103), channel_id=1, source_target_pairs={{8,0},{16,8},{24,16},{32,24},{40,32},{48,40},{56,48},{64,56},{72,6... | collective-permute-start | bytes 49160 | tf_op jit(solution)/shard_map/ppermute | solution.py:18
  390.4 5.2 %collective-permute-start.8 = (bf16[128,512]{1,0:T(8,128)(2,1)S(1)}, bf16[128,512]{1,0:T(8,128)(2,1)S(1)}, u32[]{:S(2)}, u32[]{:S(2)}) collective-permute-start(bf16[128,512]{1,0:T(8,128)(2,1)S(1)} %slice.102), channel_id=1, source_target_pairs={{8,0},{16,8},{24,16},{32,24},{40,32},{48,40},{56,48},{64,56},{72,6... | collective-permute-start | bytes 393224 | tf_op jit(solution)/shard_map/ppermute | solution.py:18
  393.2 10.6 %collective-permute-start.13 = (bf16[128,64]{0,1:T(8,128)(2,1)S(1)}, bf16[128,64]{0,1:T(8,128)(2,1)S(1)}, u32[]{:S(2)}, u32[]{:S(2)}) collective-permute-start(bf16[128,64]{0,1:T(8,128)(2,1)S(1)} %fusion.30), channel_id=1, source_target_pairs={{8,0},{16,8},{24,16},{32,24},{40,32},{48,40},{56,48},{64,56},{72,6... | collective-permute-start | bytes 49160 | tf_op jit(solution)/shard_map/ppermute | solution.py:18
  395.7 10.6 %collective-permute-start.9 = (bf16[128,512]{1,0:T(8,128)(2,1)S(1)}, bf16[128,512]{1,0:T(8,128)(2,1)S(1)}, u32[]{:S(2)}, u32[]{:S(2)}) collective-permute-start(bf16[128,512]{1,0:T(8,128)(2,1)S(1)} %fusion.21), channel_id=1, source_target_pairs={{8,0},{16,8},{24,16},{32,24},{40,32},{48,40},{56,48},{64,56},{72,6... | collective-permute-start | bytes 393224 | tf_op jit(solution)/shard_map/ppermute | solution.py:18
  403.8 10.6 %collective-permute-start.14 = (bf16[128,64]{0,1:T(8,128)(2,1)S(1)}, bf16[128,64]{0,1:T(8,128)(2,1)S(1)}, u32[]{:S(2)}, u32[]{:S(2)}) collective-permute-start(bf16[128,64]{0,1:T(8,128)(2,1)S(1)} %fusion.29), channel_id=1, source_target_pairs={{8,0},{16,8},{24,16},{32,24},{40,32},{48,40},{56,48},{64,56},{72,6... | collective-permute-start | bytes 49160 | tf_op jit(solution)/shard_map/ppermute | solution.py:18
  406.3 10.6 %collective-permute-start.10 = (bf16[128,512]{1,0:T(8,128)(2,1)S(1)}, bf16[128,512]{1,0:T(8,128)(2,1)S(1)}, u32[]{:S(2)}, u32[]{:S(2)}) collective-permute-start(bf16[128,512]{1,0:T(8,128)(2,1)S(1)} %fusion.20), channel_id=1, source_target_pairs={{8,0},{16,8},{24,16},{32,24},{40,32},{48,40},{56,48},{64,56},{72,6... | collective-permute-start | bytes 393224 | tf_op jit(solution)/shard_map/ppermute | solution.py:18
  414.4 10.5 %collective-permute-start.15 = (bf16[128,64]{0,1:T(8,128)(2,1)S(1)}, bf16[128,64]{0,1:T(8,128)(2,1)S(1)}, u32[]{:S(2)}, u32[]{:S(2)}) collective-permute-start(bf16[128,64]{0,1:T(8,128)(2,1)S(1)} %fusion.28), channel_id=1, source_target_pairs={{8,0},{16,8},{24,16},{32,24},{40,32},{48,40},{56,48},{64,56},{72,6... | collective-permute-start | bytes 49160 | tf_op jit(solution)/shard_map/ppermute | solution.py:18
  416.9 10.5 %collective-permute-start.11 = (bf16[128,512]{1,0:T(8,128)(2,1)S(1)}, bf16[128,512]{1,0:T(8,128)(2,1)S(1)}, u32[]{:S(2)}, u32[]{:S(2)}) collective-permute-start(bf16[128,512]{1,0:T(8,128)(2,1)S(1)} %fusion.19), channel_id=1, source_target_pairs={{8,0},{16,8},{24,16},{32,24},{40,32},{48,40},{56,48},{64,56},{72,6... | collective-permute-start | bytes 393224 | tf_op jit(solution)/shard_map/ppermute | solution.py:18
where the time goes:
time: 472 us; the launch traced here: 471 us
  blocking collectives  341 us (72%)
  starting transfers between devices  52.5 us (11%)
  waiting for transfers between devices  49.8 us (11%)
  matrix products  14 us (3%)
  local copies, waits for them, and re-layouts  9.54 us (2%)
    psum x1, blocking collectives, per_device(): weight_key, weight_value = lax.psum((weight_key, weight_value), 'ctx')  299 us
    ppermute x16, starting transfers between devices, from_behind(): return lax.ppermute(block, axis, route)  52.5 us
    ppermute x16, waiting for transfers between devices, from_behind(): return lax.ppermute(block, axis, route)  49.8 us
    psum x1, blocking collectives, per_device(): nope_total, rope_total = lax.psum((nope_grad, gathered_sum[1]), 'head')  42.5 us
  transfers between devices with their start and end apart: 16, of which 11 were waited for; matrix products, arithmetic and copies ran while one was open for 2% of the time, Pallas kernels for 0%

commit v1 on v0

--- a/solution.py
+++ b/solution.py
@@ -1,8 +1,11 @@
+import functools
 import math
 
 import jax
 import jax.numpy as jnp
 from jax import lax
+from jax.experimental import pallas as pl
+from jax.experimental.pallas import tpu as pltpu
 from jax.sharding import PartitionSpec as P
 
 LAT = 512
@@ -10,39 +13,446 @@
 NOPE = 128
 VDIM = 128
 PREV = 4
-
-
-def from_behind(block, axis, distance):
-    devices = range(lax.axis_size(axis))
-    route = [(i - distance, i) for i in devices if i - distance in devices]
-    return lax.ppermute(block, axis, route)
-
-
-def as_sent(shard):
-
-    def short(part):
-        return part.astype(jnp.bfloat16) if part.dtype == jnp.float32 else part
-
-    return jax.tree.map(short, shard)
+NZ = 8
+NY = 4
+MESH = pl.DeviceIdType.MESH
+
+
+def f32(x):
+    return x.astype(jnp.float32)
+
+
+def halo_kernel(n_ctx, latent_ref, window_ref, send_sem, recv_sem):
+    me = lax.axis_index("ctx")
+
+    barrier = pltpu.get_barrier_semaphore()
+    for s in range(1, PREV + 1):
+
+        @pl.when(me >= s)
+        def _():
+            pl.semaphore_signal(barrier, inc=1, device_id={"ctx": me - s}, device_id_type=MESH)
+
+    @pl.when(me < n_ctx - 1)
+    def _():
+        pl.semaphore_wait(barrier, jnp.minimum(n_ctx - 1 - me, PREV))
+
+    def copy(s):
+        return pltpu.make_async_remote_copy(
+            src_ref=latent_ref,
+            dst_ref=window_ref.at[PREV - s],
+            send_sem=send_sem.at[s - 1],
+            recv_sem=recv_sem.at[s - 1],
+            device_id={"ctx": me + s},
+            device_id_type=MESH,
+        )
+
+    for s in range(1, PREV + 1):
+
+        @pl.when(me + s < n_ctx)
+        def _():
+            copy(s).start()
+
+    window_ref[PREV] = latent_ref[...]
+    for s in range(1, PREV + 1):
+
+        @pl.when(me >= s)
+        def _():
+            copy(s).wait_recv()
+
+        @pl.when(me < s)
+        def _():
+            window_ref[PREV - s] = jnp.zeros_like(latent_ref)
+
+    for s in range(1, PREV + 1):
+
+        @pl.when(me + s < n_ctx)
+        def _():
+            copy(s).wait_send()
+
+
+def reduce_kernel(
+    n_ctx,
+    n_head,
+    gw_ref,
+    gl_ref,
+    gw_out,
+    gl_out,
+    pair_in,
+    half,
+    z_in,
+    y_in,
+    zy_in,
+    yz_in,
+    y_part,
+    z_part,
+    head_in,
+    ctx_part,
+    ctx_in,
+    pair_s,
+    pair_r,
+    pairg_s,
+    pairg_r,
+    z_s,
+    z_r,
+    y_s,
+    y_r,
+    zy_s,
+    zy_r,
+    yz_s,
+    yz_r,
+    zyg_s,
+    zyg_r,
+    yzg_s,
+    yzg_r,
+    zg_s,
+    zg_r,
+    yg_s,
+    yg_r,
+    head_s,
+    head_r,
+    ctx_s,
+    ctx_r,
+    headg_s,
+    headg_r,
+):
+    me = lax.axis_index("ctx")
+    head = lax.axis_index("head")
+    core = lax.rem(me, 2)
+    z = lax.rem(me // 2, NZ)
+    y = me // (2 * NZ)
+    partner = me + 1 - 2 * core
+    rows = gl_ref.shape[1] // n_head
+
+    def at_z(s):
+        return lax.rem(z + s, NZ)
+
+    def at_y(s):
+        return lax.rem(y + s, NY)
+
+    def z_dev(s):
+        return (y * NZ + at_z(s)) * 2 + core
+
+    def y_dev(s):
+        return (at_y(s) * NZ + z) * 2 + core
+
+    def at_head(s):
+        return lax.rem(head + s, n_head)
+
+    barrier = pltpu.get_barrier_semaphore()
+
+    def greet(device):
+        pl.semaphore_signal(barrier, inc=1, device_id=device, device_id_type=MESH)
+
+    greet({"ctx": partner})
+    for s in range(1, NZ):
+        greet({"ctx": z_dev(s)})
+    for s in range(1, NY):
+        greet({"ctx": y_dev(s)})
+    for s in range(1, n_head):
+        greet({"head": at_head(s)})
+    for s in range(1, PREV + 1):
+
+        @pl.when(me + s < n_ctx)
+        def _():
+            greet({"ctx": me + s})
+
+    pl.semaphore_wait(barrier, 1 + NZ - 1 + NY - 1 + n_head - 1 + jnp.minimum(me, PREV))
+
+    def remote(src, dst, send, recv, device):
+        return pltpu.make_async_remote_copy(
+            src_ref=src, dst_ref=dst, send_sem=send, recv_sem=recv, device_id=device, device_id_type=MESH
+        )
+
+    def mult(x, m):
+        return pl.multiple_of(x, m)
+
+    pair = remote(gw_ref.at[1 - core], pair_in, pair_s, pair_r, {"ctx": partner})
+    pair.start()
+
+    def head_copy(s):
+        return remote(
+            gl_ref.at[:, pl.ds(mult(at_head(s) * rows, rows), rows), :],
+            head_in.at[s - 1],
+            head_s.at[s - 1],
+            head_r.at[s - 1],
+            {"head": at_head(s)},
+        )
+
+    for s in range(1, n_head):
+        head_copy(s).start()
+
+    pair.wait_recv()
+    half[...] = (f32(gw_ref[core]) + f32(pair_in[...])).astype(jnp.bfloat16)
+
+    def z_copy(s):
+        return remote(
+            half.at[pl.ds(mult(at_z(s) * 32, 32), 32), :],
+            z_in.at[s - 1],
+            z_s.at[s - 1],
+            z_r.at[s - 1],
+            {"ctx": z_dev(s)},
+        )
+
+    def y_copy(s):
+        return remote(
+            half.at[pl.ds(mult(256 + at_y(s) * 64, 64), 64), :],
+            y_in.at[s - 1],
+            y_s.at[s - 1],
+            y_r.at[s - 1],
+            {"ctx": y_dev(s)},
+        )
+
+    for s in range(1, NZ):
+        z_copy(s).start()
+    for s in range(1, NY):
+        y_copy(s).start()
+
+    total = f32(gl_ref[:, pl.ds(mult(head * rows, rows), rows), :])
+    for s in range(1, n_head):
+        head_copy(s).wait_recv()
+        total += f32(head_in[s - 1])
+    ctx_part[...] = total.astype(jnp.bfloat16)
+
+    def ctx_copy(s):
+        return remote(
+            ctx_part.at[PREV - s],
+            ctx_in.at[s - 1],
+            ctx_s.at[s - 1],
+            ctx_r.at[s - 1],
+            {"ctx": me - s},
+        )
+
+    for s in range(1, PREV + 1):
+
+        @pl.when(me >= s)
+        def _():
+            ctx_copy(s).start()
+
+    total = f32(half[pl.ds(mult(z * 32, 32), 32), :])
+    for s in range(1, NZ):
+        z_copy(s).wait_recv()
+        total += f32(z_in[s - 1])
+    z_part[...] = total.astype(jnp.bfloat16)
+
+    def zy_copy(s):
+        return remote(
+            z_part.at[:, pl.ds(mult(at_y(s) * 128, 128), 128)],
+            zy_in.at[s - 1],
+            zy_s.at[s - 1],
+            zy_r.at[s - 1],
+            {"ctx": y_dev(s)},
+        )
+
+    for s in range(1, NY):
+        zy_copy(s).start()
+
+    total = f32(half[pl.ds(mult(256 + y * 64, 64), 64), :])
+    for s in range(1, NY):
+        y_copy(s).wait_recv()
+        total += f32(y_in[s - 1])
+    y_part[...] = total.astype(jnp.bfloat16)
+
+    def small(zi):
+        return pl.ds(mult(zi // 2 * 16, 16), 16), pl.ds(mult(lax.rem(zi, 2) * 256, 256), 256)
+
+    def yz_copy(s):
+        r, c = small(at_z(s))
+        return remote(
+            y_part.at[r, c],
+            yz_in.at[s - 1],
+            yz_s.at[s - 1],
+            yz_r.at[s - 1],
+            {"ctx": z_dev(s)},
+        )
+
+    for s in range(1, NZ):
+        yz_copy(s).start()
+
+    for s in range(1, PREV + 1):
+
+        @pl.when(me + s < n_ctx)
+        def _():
+            ctx_copy(s).wait_recv()
+
+        @pl.when(me + s >= n_ctx)
+        def _():
+            ctx_in[s - 1] = jnp.zeros(ctx_in.shape[1:], jnp.bfloat16)
+
+    total = f32(ctx_part[PREV])
+    for s in range(1, PREV + 1):
+        total += f32(ctx_in[s - 1])
+    my_rows = pl.ds(mult(head * rows, rows), rows)
+    gl_out[my_rows, :] = total.astype(jnp.bfloat16)
+
+    def headg_copy(s):
+        return remote(
+            gl_out.at[my_rows, :],
+            gl_out.at[my_rows, :],
+            headg_s.at[s - 1],
+            headg_r.at[s - 1],
+            {"head": at_head(s)},
+        )
+
+    for s in range(1, n_head):
+        headg_copy(s).start()
+
+    zrows = pl.ds(mult(z * 32, 32), 32)
+    ycols = pl.ds(mult(y * 128, 128), 128)
+    total = f32(z_part[:, ycols])
+    for s in range(1, NY):
+        zy_copy(s).wait_recv()
+        total += f32(zy_in[s - 1])
+    gw_out[core, zrows, ycols] = total.astype(jnp.bfloat16)
+
+    def zyg_copy(s):
+        block = gw_out.at[core, zrows, ycols]
+        return remote(block, block, zyg_s.at[s - 1], zyg_r.at[s - 1], {"ctx": y_dev(s)})
+
+    for s in range(1, NY):
+        zyg_copy(s).start()
+
+    r, c = small(z)
+    total = f32(y_part[r, c])
+    for s in range(1, NZ):
+        yz_copy(s).wait_recv()
+        total += f32(yz_in[s - 1])
+    brows = pl.ds(mult(256 + y * 64 + z // 2 * 16, 16), 16)
+    gw_out[core, brows, c] = total.astype(jnp.bfloat16)
+
+    def yzg_copy(s):
+        block = gw_out.at[core, brows, c]
+        return remote(block, block, yzg_s.at[s - 1], yzg_r.at[s - 1], {"ctx": z_dev(s)})
+
+    for s in range(1, NZ):
+        yzg_copy(s).start()
+
+    for s in range(1, NY):
+        zyg_copy(s).wait_recv()
+
+    def zg_copy(s):
+        block = gw_out.at[core, zrows, :]
+        return remote(block, block, zg_s.at[s - 1], zg_r.at[s - 1], {"ctx": z_dev(s)})
+
+    for s in range(1, NZ):
+        zg_copy(s).start()
+
+    for s in range(1, NZ):
+        yzg_copy(s).wait_recv()
+
+    def yg_copy(s):
+        block = gw_out.at[core, pl.ds(mult(256 + y * 64, 64), 64), :]
+        return remote(block, block, yg_s.at[s - 1], yg_r.at[s - 1], {"ctx": y_dev(s)})
+
+    for s in range(1, NY):
+        yg_copy(s).start()
+
+    for s in range(1, NZ):
+        zg_copy(s).wait_recv()
+    for s in range(1, NY):
+        yg_copy(s).wait_recv()
+    block = gw_out.at[core]
+    pairg = remote(block, block, pairg_s, pairg_r, {"ctx": partner})
+    pairg.start()
+    pair.wait_send()
+
+    for s in range(1, n_head):
+        head_copy(s).wait_send()
+        headg_copy(s).wait()
+    for s in range(1, NZ):
+        z_copy(s).wait_send()
+        yz_copy(s).wait_send()
+        yzg_copy(s).wait_send()
+        zg_copy(s).wait_send()
+    for s in range(1, NY):
+        y_copy(s).wait_send()
+        zy_copy(s).wait_send()
+        zyg_copy(s).wait_send()
+        yg_copy(s).wait_send()
+    for s in range(1, PREV + 1):
+
+        @pl.when(me >= s)
+        def _():
+            ctx_copy(s).wait_send()
+
+    pairg.wait()
+
+
+VMEM_SPEC = pl.BlockSpec(memory_space=pltpu.VMEM)
+
+
+def halo(latent, n_ctx):
+    tok, wide = latent.shape
+    return pl.pallas_call(
+        functools.partial(halo_kernel, n_ctx),
+        out_shape=jax.ShapeDtypeStruct((PREV + 1, tok, wide), latent.dtype),
+        in_specs=[VMEM_SPEC],
+        out_specs=VMEM_SPEC,
+        scratch_shapes=[pltpu.SemaphoreType.DMA((PREV,)), pltpu.SemaphoreType.DMA((PREV,))],
+        compiler_params=pltpu.CompilerParams(collective_id=0, has_side_effects=True),
+        name="halo",
+    )(latent)
+
+
+def reduce_all(gw, gl, n_ctx, n_head):
+    tok, wide = gl.shape[1:]
+    rows = tok // n_head
+    bf = jnp.bfloat16
+
+    def sems(n):
+        return [pltpu.SemaphoreType.DMA((n,)), pltpu.SemaphoreType.DMA((n,))]
+
+    return pl.pallas_call(
+        functools.partial(reduce_kernel, n_ctx, n_head),
+        out_shape=[
+            jax.ShapeDtypeStruct(gw.shape, bf),
+            jax.ShapeDtypeStruct((tok, wide), bf),
+        ],
+        in_specs=[VMEM_SPEC] * 2,
+        out_specs=[VMEM_SPEC] * 2,
+        scratch_shapes=[
+            pltpu.VMEM((512, 512), bf),
+            pltpu.VMEM((512, 512), bf),
+            pltpu.VMEM((NZ - 1, 32, 512), bf),
+            pltpu.VMEM((NY - 1, 64, 512), bf),
+            pltpu.VMEM((NY - 1, 32, 128), bf),
+            pltpu.VMEM((NZ - 1, 16, 256), bf),
+            pltpu.VMEM((64, 512), bf),
+            pltpu.VMEM((32, 512), bf),
+            pltpu.VMEM((n_head - 1, PREV + 1, rows, wide), bf),
+            pltpu.VMEM((PREV + 1, rows, wide), bf),
+            pltpu.VMEM((PREV, rows, wide), bf),
+            *[pltpu.SemaphoreType.DMA] * 4,
+            *sems(NZ - 1),
+            *sems(NY - 1),
+            *sems(NY - 1),
+            *sems(NZ - 1),
+            *sems(NY - 1),
+            *sems(NZ - 1),
+            *sems(NZ - 1),
+            *sems(NY - 1),
+            *sems(n_head - 1),
+            *sems(PREV),
+            *sems(n_head - 1),
+        ],
+        compiler_params=pltpu.CompilerParams(
+            collective_id=1, has_side_effects=True, vmem_limit_bytes=32 * 2**20
+        ),
+        name="reduce_all",
+    )(gw, gl)
 
 
 def per_device(queries, latent, w_key, w_value, grad_out, segment_ids):
     tok_rows = queries.shape[0]
     head_count = w_key.shape[1] // NOPE
+    n_ctx = lax.axis_size("ctx")
+    n_head = lax.axis_size("head")
     window = (PREV + 1) * tok_rows
     margin = PREV * tok_rows
     scale_factor = 1.0 / math.sqrt(NOPE + ROPE)
     position = lax.axis_index("ctx")
-    latent_nope = latent[:, :LAT]
-    own_block = (latent_nope, latent[:, LAT:])
-    arrived = [own_block]
-    moving = own_block
-    for distance in range(PREV):
-        moving = from_behind((moving[0], moving[1]), "ctx", 1)
-        arrived.append(moving)
-    ordered = arrived[::-1]
-    first_part = jnp.concatenate([element[0] for element in ordered], 0)
-    window_rope = jnp.concatenate([element[1] for element in ordered], 0)
+    window_all = halo(latent, n_ctx).reshape(window, LAT + ROPE)
+    first_part = window_all[:, :LAT]
+    window_rope = window_all[:, LAT:]
     key_flat = jnp.dot(first_part, w_key, preferred_element_type=jnp.float32).astype(jnp.bfloat16)
     value_flat = jnp.dot(first_part, w_value, preferred_element_type=jnp.float32).astype(
         jnp.bfloat16
@@ -115,37 +525,14 @@
     )
     weight_key = jnp.dot(first_part.T, nope_flat, preferred_element_type=jnp.float32)
     weight_value = jnp.dot(first_part.T, value_flat_grad, preferred_element_type=jnp.float32)
-    pieces = [
-        (
-            first_term[offset * tok_rows : (offset + 1) * tok_rows],
-            rope_term[offset * tok_rows : (offset + 1) * tok_rows],
-        )
-        for offset in range(PREV + 1)
-    ]
-    gathered_sum = pieces[0]
-    for distance in range(PREV):
-        incoming = jax.tree.map(
-            lambda part, own: part.astype(own.dtype),
-            from_behind(as_sent(gathered_sum), "ctx", -1),
-            gathered_sum,
-        )
-        gathered_sum = (
-            incoming[0] + pieces[distance + 1][0],
-            incoming[1] + pieces[distance + 1][1],
-        )
-    nope_grad = gathered_sum[0]
-    nope_total, rope_total = lax.psum((nope_grad, gathered_sum[1]), "head")
-    weight_key, weight_value = lax.psum((weight_key, weight_value), "ctx")
-    grad_latent = jnp.concatenate([nope_total, rope_total], 1).astype(jnp.bfloat16)
+    gw = jnp.stack([weight_key.astype(jnp.bfloat16), weight_value.astype(jnp.bfloat16)])
+    gl = jnp.concatenate([first_term, rope_term], 1).astype(jnp.bfloat16)
+    gw_sum, grad_latent = reduce_all(
+        gw, gl.reshape(PREV + 1, tok_rows, LAT + ROPE), n_ctx, n_head
+    )
     attn_out = attn_block.reshape(tok_rows, head_count * VDIM)
     grad_queries = grad_query.astype(jnp.bfloat16).reshape(tok_rows, head_count * (NOPE + ROPE))
-    return (
-        attn_out,
-        grad_queries,
-        grad_latent,
-        weight_key.astype(jnp.bfloat16),
-        weight_value.astype(jnp.bfloat16),
-    )
+    return (attn_out, grad_queries, grad_latent, gw_sum[0], gw_sum[1])
 
 
 def solution(mesh):

time: 472 us -> 112 us (0.24)
  the two profiles are of different devices: /device:TPU:32 before, /device:TPU:1 now
where the time goes in v1:
time: 112 us
  Pallas kernels  83.1 us (74%)
  matrix products  15.8 us (14%)
  local copies, waits for them, and re-layouts  8.96 us (8%)
  other arithmetic  2.77 us (2%)
    pallas_call x1, Pallas kernels, reduce_all(): pl.pallas_call(functools.partial(reduce_kernel, n_ctx, n_head), out_shape...  62.3 us
    pallas_call x1, Pallas kernels, halo(): pl.pallas_call(functools.partial(halo_kernel, n_ctx), out_shape=jax.Shape...  20.8 us
    unnamed x30, local copies, waits for them, and re-layouts  7.69 us
    dot_general x1, matrix products, per_device(): jnp.einsum('htw,thd->whd', probability.astype(jnp.bfloat16), upstream, pr...  2.42 us

profile of v1, /device:TPU:1, one launch (start us, length us, event | category | flops | bytes accessed | tf_op | source)
XLA Modules:
  0.0 111.5 jit_solution(8295666313143566909)
XLA Ops:
  0.6 0.0 copy-start
  0.6 1.7 %copy.57 = bf16[128,512]{0,1:T(8,128)(2,1)} copy(bf16[128,512]{1,0:T(8,128)(2,1)} %param.10) | data formatting | bytes 262144 | tf_op args[4]
  2.4 1.7 %copy.51.latent_ref = bf16[128,576]{1,0:T(8,128)(2,1)} copy(bf16[128,576]{0,1:T(8,128)(2,1)} %param.7) | data formatting | bytes 294912 | tf_op args[1]
  4.1 0.0 copy-start.10
  4.1 20.8 %halo.1 = bf16[5,128,576]{2,1,0:T(8,128)(2,1)} custom-call(bf16[128,576]{1,0:T(8,128)(2,1)} %copy.51.latent_ref), custom_call_target="tpu_custom_call" | custom-call | tf_op jit(solution)/shard_map/halo/pallas_call | solution.py:385
  24.9 0.0 copy-done
  24.9 1.7 %convolution_convert_fusion.2 = bf16[640,512]{0,1:T(8,128)(2,1)S(1)} fusion(bf16[512,512]{1,0:T(8,128)(2,1)S(1)} %copy-done, bf16[640,576]{1,0:T(8,128)(2,1)} %bitcast.88), kind=kOutput, calls=%fused_computation.19 | convolution fusion | flops 335872000 | bytes 1835008 | tf_op jit(solution)/shard_map/dot_general | solution.py:456
  26.6 0.0 copy-start.1
  26.6 0.0 copy-start.11
  26.6 0.0 copy-done.10
  26.6 0.2 copy.52
  26.8 0.4 convolution_bitcast_fusion.1
  27.2 0.2 copy-done.11
  27.4 0.1 dynamic_slice.7
  27.5 0.1 pad_dynamic-slice_fusion
  27.6 0.0 copy-done.1
  27.6 0.3 compare_and_fusion
  27.9 0.0 copy-start.5
  27.9 1.3 %fusion.6 = f32[4,128,640]{1,2,0:T(8,128)S(1)} fusion(f32[4,128,640]{1,2,0:T(8,128)S(1)} %convolution_bitcast_fusion.1, pred[128,640]{0,1:T(8,128)(4,1)S(1)} %compare_and_fusion, bf16[640,576]{1,0:T(8,128)(2,1)} %bitcast.89, bf16[128,4,192]{0,2,1:T(8,128)(2,1)S(1)} %bitcast.95), kind=kOutput, calls=%fused_computation.9 | convolution fusion | flops 42926080 | bytes 2932736 | tf_op jit(solution)/shard_map/thd,wd->htw/dot_general | solution.py:479
  29.2 0.0 copy-done.5
  29.2 0.0 copy-start.3
  29.2 0.0 copy-start.8
  29.2 1.5 %fusion.33 = (f32[4,128]{1,0:T(4,128)S(1)}, f32[4,128,640]{1,2,0:T(8,128)}) fusion(f32[4,128,640]{1,2,0:T(8,128)S(1)} %fusion.6, pred[128,640]{0,1:T(8,128)(4,1)S(1)} %compare_and_fusion), kind=kOutput, calls=%fused_computation.60 | output fusion | flops 983679 | bytes 2705408 | tf_op jit(solution)/shard_map/sub | solution.py:483
  30.7 0.0 copy-start.6
  30.7 0.0 copy-done.3
  30.7 0.0 copy-done.8
  30.7 1.5 %convolution_convert_fusion.1 = bf16[640,512]{0,1:T(8,128)(2,1)} fusion(bf16[512,512]{1,0:T(8,128)(2,1)S(1)} %copy-done.8, bf16[640,576]{1,0:T(8,128)(2,1)S(1)} %bitcast.90), kind=kOutput, calls=%fused_computation.18 | convolution fusion | flops 335872000 | bytes 1835008 | tf_op jit(solution)/shard_map/dot_general | solution.py:457
  32.2 0.0 copy-done.6
  32.2 1.7 %multiply_reduce_fusion = (f32[128,4]{0,1:T(4,128)S(1)}, bf16[128,4,128]{0,2,1:T(8,128)(2,1)S(1)}) fusion(bf16[128,512]{0,1:T(8,128)(2,1)} %copy.57, f32[128,4]{0,1:T(4,128)S(1)} %bitcast.105, bf16[640,4,128]{0,2,1:T(8,128)(2,1)} %bitcast.106, f32[4,128,640]{1,2,0:T(8,128)S(1)} %fusion.6, pred[128,640]{0,1:T(8,128)(4,1)S(1)} %copy-done.6), kind=kOutput, calls=%fused_computation.46 | convolution fusion | flops 85262976 | bytes 2314240 | tf_op jit(solution)/shard_map/htw,whd->htd/dot_general | solution.py:487
  33.8 0.8 copy.69
  34.6 0.0 copy-start.2
  34.6 2.0 %fusion.10 = bf16[4,128,640]{1,2,0:T(8,128)(2,1)S(1)} fusion(bf16[640,4,128]{0,2,1:T(8,128)(2,1)} %bitcast.107, bf16[128,4,128]{0,2,1:T(8,128)(2,1)} %bitcast.102, f32[4,128]{1,0:T(4,128)S(1)} %bitcast.108, f32[4,128,640]{1,2,0:T(8,128)} %get-tuple-element.27, f32[4,128]{1,0:T(4,128)S(1)} %get-tuple-element.26), kind=kOutput, calls=%fused_computation.15 | convolution fusion | flops 85196800 | bytes 2756608 | tf_op jit(solution)/shard_map/thd,whd->htw/dot_general | solution.py:495
  36.6 0.2 convolution_bitcast_fusion.4
  36.9 0.0 copy-done.2
  36.9 0.3 convolution_bitcast_fusion.3
  37.2 0.7 fusion.24
  38.0 1.7 %copy.70 = bf16[128,768]{1,0:T(8,128)(2,1)} copy(bf16[128,768]{0,1:T(8,128)(2,1)} %bitcast.98) | data formatting | bytes 393216
  39.7 2.4 %convolution_convert_fusion = bf16[4,640,128]{1,2,0:T(8,128)(2,1)} fusion(bf16[128,4,128]{0,2,1:T(8,128)(2,1)} %bitcast.103, f32[4,128]{1,0:T(4,128)S(1)} %get-tuple-element.26, f32[4,128,640]{1,2,0:T(8,128)S(1)} %fusion.6, pred[128,640]{0,1:T(8,128)(4,1)} %copy-done.5), kind=kOutput, calls=%fused_computation.17 | convolution fusion | flops 85525632 | bytes 2181120 | tf_op jit(solution)/shard_map/htw,thd->whd/dot_general | solution.py:514
  42.1 0.0 copy-start.4
  42.1 1.8 %fusion.13 = bf16[1,512,512]{2,1,0:T(8,128)(2,1)S(1)} fusion(bf16[640,512]{0,1:T(8,128)(2,1)} %bitcast.100, bf16[640,576]{1,0:T(8,128)(2,1)S(1)} %bitcast.92), kind=kOutput, calls=%fused_computation.24 | convolution fusion | flops 335806464 | bytes 1835008 | tf_op jit(solution)/shard_map/dot_general | solution.py:527
  43.9 0.4 fusion.11
  44.3 0.0 copy-done.4
  44.3 0.6 fusion.12
  44.9 0.1 pad_maximum_fusion.gw_ref
  45.0 0.4 fusion.16
  45.4 0.0 copy-start.7
  45.4 0.2 copy.68
  45.6 0.0 copy-start.9
  45.6 0.6 fusion.34
  46.2 0.3 copy-done.7
  46.5 0.2 copy-done.9
  46.7 0.6 fusion.9
  47.3 0.1 pad_maximum_fusion.1.gl_ref
  47.3 62.3 %reduce_all.1 = (bf16[2,512,512]{2,1,0:T(8,128)(2,1)S(1)}, bf16[128,576]{1,0:T(8,128)(2,1)S(1)}) custom-call(bf16[2,512,512]{2,1,0:T(8,128)(2,1)S(1)} %pad_maximum_fusion.gw_ref, bf16[5,128,576]{2,1,0:T(8,128)(2,1)S(1)} %pad_maximum_fusion.1.gl_ref), custom_call_target="tpu_custom_call" | custom-call | tf_op jit(solution)/shard_map/reduce_all/pallas_call | solution.py:404
  109.7 0.8 copy.71
  110.5 1.0 slice_bitcast_fusion
  (2 shorter events, 0.0 us)
Async XLA Ops:
  0.6 24.3 %copy-start = (bf16[512,512]{1,0:T(8,128)(2,1)S(1)}, bf16[512,512]{1,0:T(8,128)(2,1)}, u32[]{:S(2)}) copy-start(bf16[512,512]{1,0:T(8,128)(2,1)} %param.8) | copy-start | bytes 1572868
  4.1 22.6 %copy-start.10 = (bf16[128,768]{1,0:T(8,128)(2,1)S(1)}, bf16[128,768]{1,0:T(8,128)(2,1)}, u32[]{:S(2)}) copy-start(bf16[128,768]{1,0:T(8,128)(2,1)} %param.6) | copy-start | bytes 589828
  26.6 1.0 copy-start.1
  26.6 0.8 copy-start.11
  27.9 1.3 %copy-start.5 = (pred[128,640]{0,1:T(8,128)(4,1)}, pred[128,640]{0,1:T(8,128)(4,1)S(1)}, u32[]{:S(2)}) copy-start(pred[128,640]{0,1:T(8,128)(4,1)S(1)} %compare_and_fusion) | copy-start | bytes 245764
  29.2 1.5 %copy-start.3 = (bf16[5,128,576]{2,1,0:T(8,128)(2,1)S(1)}, bf16[5,128,576]{2,1,0:T(8,128)(2,1)}, u32[]{:S(2)}) copy-start(bf16[5,128,576]{2,1,0:T(8,128)(2,1)} %halo.1) | copy-start | bytes 2211844
  29.2 1.5 %copy-start.8 = (bf16[512,512]{1,0:T(8,128)(2,1)S(1)}, bf16[512,512]{1,0:T(8,128)(2,1)}, u32[]{:S(2)}) copy-start(bf16[512,512]{1,0:T(8,128)(2,1)} %param.9) | copy-start | bytes 1572868
  30.7 1.5 %copy-start.6 = (pred[128,640]{0,1:T(8,128)(4,1)S(1)}, pred[128,640]{0,1:T(8,128)(4,1)}, u32[]{:S(2)}) copy-start(pred[128,640]{0,1:T(8,128)(4,1)} %copy-done.5) | copy-start | bytes 245764
  34.6 2.3 %copy-start.2 = (bf16[640,512]{0,1:T(8,128)(2,1)S(1)}, bf16[640,512]{0,1:T(8,128)(2,1)}, u32[]{:S(2)}) copy-start(bf16[640,512]{0,1:T(8,128)(2,1)} %copy-done.1) | copy-start | bytes 1966084
  42.1 2.2 %copy-start.4 = (bf16[5,128,576]{2,1,0:T(8,128)(2,1)S(1)}, bf16[5,128,576]{2,1,0:T(8,128)(2,1)}, u32[]{:S(2)}) copy-start(bf16[5,128,576]{2,1,0:T(8,128)(2,1)} %halo.1) | copy-start | bytes 2211844
  45.4 1.1 copy-start.7
  45.6 1.1 copy-start.9

commit v2 on v0

v2 whole, which is shorter than its diff:
```python
import functools
import math

import jax
import jax.numpy as jnp
from jax import lax
from jax.experimental import pallas as pl
from jax.experimental.pallas import tpu as pltpu
from jax.sharding import PartitionSpec as P

LAT = 512
ROPE = 64
NOPE = 128
VDIM = 128
PREV = 4
NZ = 8
NY = 4
TOK = 128
WIN = (PREV + 1) * TOK
QK = NOPE + ROPE
HEADS = 4
PIECES = 2
COLS = HEADS // PIECES * NOPE
MESH = pl.DeviceIdType.MESH
BF = jnp.bfloat16
SCALE = 1.0 / math.sqrt(QK)


def f32(x):
    return x.astype(jnp.float32)


def nn(a, b):
    return jnp.dot(a, b, preferred_element_type=jnp.float32)


def nt(a, b):
    return lax.dot_general(a, b, (((1,), (1,)), ((), ())), preferred_element_type=jnp.float32)


def mult(x, m):
    return pl.multiple_of(x, m)


def slot_cols(slot):
    return pl.ds(slot * TOK, TOK)


def kernel(n_ctx, n_head, *refs):
    (
        q_hbm,
        lat_ref,
        wk_hbm,
        wv_hbm,
        do_hbm,
        seg_ref,
        attn_ref,
        gq_ref,
        gl_out,
        gw_out,
        q_ref,
        wcat,
        do_ref,
        win,
        wt,
        qs,
        qt,
        dot,
        kt,
        vt,
        bias,
        dcat,
        rope_sum,
        part,
        pair_in,
        half,
        z_in,
        y_in,
        zy_in,
        yz_in,
        z_part,
        y_part,
        glb,
        head_in,
        ctx_part,
        ctx_in,
        load_sem,
        halo_s,
        halo_r,
        mate_s,
        mate_r,
        pair_s,
        pair_r,
        z_s,
        z_r,
        y_s,
        y_r,
        zy_s,
        zy_r,
        yz_s,
        yz_r,
        zyg_s,
        zyg_r,
        yzg_s,
        yzg_r,
        zg_s,
        zg_r,
        yg_s,
        yg_r,
        pairg_s,
        pairg_r,
        head_s,
        head_r,
        ctx_s,
        ctx_r,
        headg_s,
        headg_r,
    ) = refs
    me = lax.axis_index("ctx")
    head = lax.axis_index("head")
    core = lax.rem(me, 2)
    z = lax.rem(me // 2, NZ)
    y = me // (2 * NZ)
    partner = me + 1 - 2 * core
    rows = glb.shape[0] // n_head

    def z_dev(s):
        return {"ctx": (y * NZ + lax.rem(z + s, NZ)) * 2 + core}

    def y_dev(s):
        return {"ctx": (lax.rem(y + s, NY) * NZ + z) * 2 + core}

    def at_head(s):
        return lax.rem(head + s, n_head)

    def remote(src, dst, send, recv, device):
        return pltpu.make_async_remote_copy(
            src_ref=src, dst_ref=dst, send_sem=send, recv_sem=recv, device_id=device, device_id_type=MESH
        )

    loads = [
        pltpu.make_async_copy(src, dst, load_sem.at[i])
        for i, (src, dst) in enumerate(
            [(q_hbm, q_ref), (do_hbm, do_ref)]
            + [
                (w.at[:, pl.ds(p * COLS, COLS)], wcat.at[:, pl.ds((2 * p + kind) * COLS, COLS)])
                for p in range(PIECES)
                for kind, w in enumerate((wk_hbm, wv_hbm))
            ]
        )
    ]
    for load in loads:
        load.start()

    barrier = pltpu.get_barrier_semaphore()

    def greet(device):
        pl.semaphore_signal(barrier, inc=1, device_id=device, device_id_type=MESH)

    for s in range(1, PREV + 1):

        @pl.when(me >= s)
        def _():
            greet({"ctx": me - s})

        @pl.when(me + s < n_ctx)
        def _():
            greet({"ctx": me + s})

    greet({"ctx": partner})
    for s in range(1, NZ):
        greet(z_dev(s))
    for s in range(1, NY):
        greet(y_dev(s))
    for s in range(1, n_head):
        greet({"head": at_head(s)})
    pl.semaphore_wait(
        barrier,
        NZ - 1 + NY - 1 + n_head + jnp.minimum(me, PREV) + jnp.minimum(n_ctx - 1 - me, PREV),
    )

    def halo_copy(i):
        d = 2 * (i + 1)
        return remote(
            lat_ref, win.at[:, slot_cols(PREV - d)], halo_s.at[i], halo_r.at[i], {"ctx": me + d}
        )

    def mate_copy(i, src):
        return remote(
            src, win.at[:, slot_cols(PREV - 1 - 2 * i)], mate_s.at[i], mate_r.at[i], {"ctx": partner}
        )

    for i in range(2):

        @pl.when(me + 2 * (i + 1) < n_ctx)
        def _():
            halo_copy(i).start()

    @pl.when(core == 0)
    def _():
        mate_copy(0, lat_ref).start()

    win[:, slot_cols(PREV)] = lat_ref[...]
    for load in loads:
        load.wait()
    for i in range(2 * PIECES):
        wt[pl.ds(i * COLS, COLS), :] = wcat[:, pl.ds(i * COLS, COLS)].T
    for h in range(HEADS):
        block = q_ref[:, pl.ds(h * QK, QK)]
        qs[h] = block
        qt[h] = block.T
        dot[h] = do_ref[:, pl.ds(h * VDIM, VDIM)].T
    own = seg_ref[pl.ds(me, 1), :]
    query_seg = jnp.broadcast_to(own, (TOK, TOK)).T
    for s in range(PREV + 1):
        place = me - PREV + s
        key_seg = jnp.where(place >= 0, seg_ref[pl.ds(jnp.maximum(place, 0), 1), :], -1)
        allowed = query_seg == key_seg
        if s == PREV:
            allowed &= lax.broadcasted_iota(jnp.int32, (TOK, TOK), 1) <= lax.broadcasted_iota(
                jnp.int32, (TOK, TOK), 0
            )
        bias[:, slot_cols(s)] = jnp.where(allowed, 0.0, -jnp.inf)

    def project(start, size):
        cols = pl.ds(start, size)
        for h in range(HEADS):
            p, j = divmod(h, HEADS // PIECES)
            base = 2 * p * COLS + j * NOPE
            kt[h, pl.ds(0, NOPE), cols] = nn(wt[pl.ds(base, NOPE), :], win[pl.ds(0, LAT), cols]).astype(BF)
            kt[h, pl.ds(NOPE, ROPE), cols] = win[pl.ds(LAT, ROPE), cols]
            vt[h, :, cols] = nn(wt[pl.ds(base + COLS, NOPE), :], win[pl.ds(0, LAT), cols]).astype(BF)

    project(PREV * TOK, TOK)

    def arrived(i):
        d = 2 * (i + 1)

        @pl.when(me >= d)
        def _():
            halo_copy(i).wait_recv()

        @pl.when(me < d)
        def _():
            win[:, slot_cols(PREV - d)] = jnp.zeros((LAT + ROPE, TOK), BF)

    arrived(0)

    @pl.when(core == 0)
    def _():
        mate_copy(1, win.at[:, slot_cols(2)]).start()

    @pl.when(core == 1)
    def _():
        mate_copy(0, win.at[:, slot_cols(2)]).start()

    arrived(1)

    @pl.when(core == 1)
    def _():
        mate_copy(1, win.at[:, slot_cols(0)]).start()

    for i in range(2):
        mate_copy(i, lat_ref).wait_recv()
    project(0, PREV * TOK)

    def one_head(h):
        p, j = divmod(h, HEADS // PIECES)
        base = 2 * p * COLS + j * NOPE
        scores = nn(qs[h], kt[h]) * SCALE + bias[...]
        expo = jnp.exp(scores - jnp.max(scores, axis=1, keepdims=True))
        scaling = 1.0 / jnp.sum(expo, axis=1, keepdims=True)
        out = (nt(expo.astype(BF), vt[h]) * scaling).astype(BF)
        attn_ref[:, pl.ds(h * VDIM, VDIM)] = out
        upstream = do_ref[:, pl.ds(h * VDIM, VDIM)]
        delta = jnp.sum(f32(upstream) * f32(out), axis=1, keepdims=True)
        probs = expo * scaling
        grad_scores = (probs * (nn(upstream, vt[h]) - delta)).astype(BF)
        gq_ref[:, pl.ds(h * QK, QK)] = (nt(grad_scores, kt[h]) * SCALE).astype(BF)
        term = (nn(qt[h], grad_scores) * SCALE).astype(BF)
        dcat[pl.ds(base, NOPE), :] = term[:NOPE]
        rope_sum[...] = f32(term[NOPE:]) if h == 0 else rope_sum[...] + f32(term[NOPE:])
        dcat[pl.ds(base + COLS, VDIM), :] = nn(dot[h], probs.astype(BF)).astype(BF)

    def pair_copy(p):
        return remote(
            part.at[p, 1 - core], pair_in.at[p], pair_s.at[p], pair_r.at[p], {"ctx": partner}
        )

    def weight_terms(p):
        terms = nt(win[pl.ds(0, LAT), :], dcat[pl.ds(2 * p * COLS, 2 * COLS), :]).astype(BF)
        part[p, 0] = terms[:, :COLS]
        part[p, 1] = terms[:, COLS:]
        pair_copy(p).start()

    def z_copy(p, s):
        block = pl.ds(mult(lax.rem(z + s, NZ) * 32, 32), 32)
        return remote(half.at[p, block], z_in.at[p, s - 1], z_s.at[p, s - 1], z_r.at[p, s - 1], z_dev(s))

    def y_copy(p, s):
        block = pl.ds(mult(256 + lax.rem(y + s, NY) * 64, 64), 64)
        return remote(half.at[p, block], y_in.at[p, s - 1], y_s.at[p, s - 1], y_r.at[p, s - 1], y_dev(s))

    def small(i):
        return pl.ds(mult(i // 2 * 16, 16), 16), pl.ds(mult(lax.rem(i, 2) * 128, 128), 128)

    def zy_copy(p, s):
        r, c = small(lax.rem(y + s, NY))
        return remote(z_part.at[p, r, c], zy_in.at[p, s - 1], zy_s.at[p, s - 1], zy_r.at[p, s - 1], y_dev(s))

    def yz_copy(p, s):
        r, c = small(lax.rem(z + s, NZ))
        return remote(y_part.at[p, r, c], yz_in.at[p, s - 1], yz_s.at[p, s - 1], yz_r.at[p, s - 1], z_dev(s))

    def z_place(p):
        return gw_out.at[core, pl.ds(mult(z * 32, 32), 32), pl.ds(p * COLS, COLS)]

    def y_place(p):
        return gw_out.at[core, pl.ds(mult(256 + y * 64, 64), 64), pl.ds(p * COLS, COLS)]

    def zy_place(p):
        r = pl.ds(mult(z * 32 + y // 2 * 16, 16), 16)
        return gw_out.at[core, r, pl.ds(mult(p * COLS + lax.rem(y, 2) * 128, 128), 128)]

    def yz_place(p):
        r = pl.ds(mult(256 + y * 64 + z // 2 * 16, 16), 16)
        return gw_out.at[core, r, pl.ds(mult(p * COLS + lax.rem(z, 2) * 128, 128), 128)]

    def zyg_copy(p, s):
        return remote(zy_place(p), zy_place(p), zyg_s.at[p, s - 1], zyg_r.at[p, s - 1], y_dev(s))

    def yzg_copy(p, s):
        return remote(yz_place(p), yz_place(p), yzg_s.at[p, s - 1], yzg_r.at[p, s - 1], z_dev(s))

    def zg_copy(p, s):
        return remote(z_place(p), z_place(p), zg_s.at[p, s - 1], zg_r.at[p, s - 1], z_dev(s))

    def yg_copy(p, s):
        return remote(y_place(p), y_place(p), yg_s.at[p, s - 1], yg_r.at[p, s - 1], y_dev(s))

    def pairg_copy(p):
        block = gw_out.at[core, :, pl.ds(p * COLS, COLS)]
        return remote(block, block, pairg_s.at[p], pairg_r.at[p], {"ctx": partner})

    def stage_a(p):
        pair_copy(p).wait_recv()
        half[p] = (f32(part[p, core]) + f32(pair_in[p])).astype(BF)
        for s in range(1, NZ):
            z_copy(p, s).start()
        for s in range(1, NY):
            y_copy(p, s).start()

    def stage_b(p):
        total = f32(half[p, pl.ds(mult(z * 32, 32), 32), :])
        for s in range(1, NZ):
            z_copy(p, s).wait_recv()
            total += f32(z_in[p, s - 1])
        z_part[p] = total.astype(BF)
        for s in range(1, NY):
            zy_copy(p, s).start()
        total = f32(half[p, pl.ds(mult(256 + y * 64, 64), 64), :])
        for s in range(1, NY):
            y_copy(p, s).wait_recv()
            total += f32(y_in[p, s - 1])
        y_part[p] = total.astype(BF)
        for s in range(1, NZ):
            yz_copy(p, s).start()

    def stage_c(p):
        r, c = small(y)
        total = f32(z_part[p, r, c])
        for s in range(1, NY):
            zy_copy(p, s).wait_recv()
            total += f32(zy_in[p, s - 1])
        zy_place(p)[...] = total.astype(BF)
        for s in range(1, NY):
            zyg_copy(p, s).start()
        r, c = small(z)
        total = f32(y_part[p, r, c])
        for s in range(1, NZ):
            yz_copy(p, s).wait_recv()
            total += f32(yz_in[p, s - 1])
        yz_place(p)[...] = total.astype(BF)
        for s in range(1, NZ):
            yzg_copy(p, s).start()

    def stage_d(p):
        for s in range(1, NY):
            zyg_copy(p, s).wait_recv()
        for s in range(1, NZ):
            zg_copy(p, s).start()
        for s in range(1, NZ):
            yzg_copy(p, s).wait_recv()
        for s in range(1, NY):
            yg_copy(p, s).start()

    def stage_e(p):
        for s in range(1, NZ):
            zg_copy(p, s).wait_recv()
        for s in range(1, NY):
            yg_copy(p, s).wait_recv()
        pairg_copy(p).start()

    def head_copy(s):
        block = pl.ds(mult(at_head(s) * rows, 16), rows)
        return remote(
            glb.at[block], head_in.at[s - 1], head_s.at[s - 1], head_r.at[s - 1], {"head": at_head(s)}
        )

    def ctx_copy(s):
        return remote(
            ctx_part.at[:, slot_cols(PREV - s)],
            ctx_in.at[s - 1],
            ctx_s.at[s - 1],
            ctx_r.at[s - 1],
            {"ctx": me - s},
        )

    def headg_copy(s):
        block = gl_out.at[pl.ds(mult(head * rows, 16), rows)]
        return remote(block, block, headg_s.at[s - 1], headg_r.at[s - 1], {"head": at_head(s)})

    def latent_terms():
        glb[pl.ds(0, LAT), :] = nn(wcat[...], dcat[...]).astype(BF)
        glb[pl.ds(LAT, ROPE), :] = rope_sum[...].astype(BF)
        glb[pl.ds(LAT + ROPE, glb.shape[0] - LAT - ROPE), :] = jnp.zeros(
            (glb.shape[0] - LAT - ROPE, WIN), BF
        )
        for s in range(1, n_head):
            head_copy(s).start()

    def latent_heads():
        total = f32(glb[pl.ds(mult(head * rows, 16), rows), :])
        for s in range(1, n_head):
            head_copy(s).wait_recv()
            total += f32(head_in[s - 1])
        ctx_part[...] = total.astype(BF)
        for s in range(1, PREV + 1):

            @pl.when(me >= s)
            def _():
                ctx_copy(s).start()

    def latent_blocks():
        for s in range(1, PREV + 1):

            @pl.when(me + s < n_ctx)
            def _():
                ctx_copy(s).wait_recv()

            @pl.when(me + s >= n_ctx)
            def _():
                ctx_in[s - 1] = jnp.zeros(ctx_in.shape[1:], BF)

        total = f32(ctx_part[:, slot_cols(PREV)])
        for s in range(1, PREV + 1):
            total += f32(ctx_in[s - 1])
        gl_out[pl.ds(mult(head * rows, 16), rows), :] = total.astype(BF)
        for s in range(1, n_head):
            headg_copy(s).start()

    one_head(0)
    one_head(1)
    weight_terms(0)
    one_head(2)
    stage_a(0)
    one_head(3)
    weight_terms(1)
    latent_terms()
    stage_a(1)
    stage_b(0)
    latent_heads()
    stage_b(1)
    stage_c(0)
    latent_blocks()
    stage_c(1)
    stage_d(0)
    stage_d(1)
    stage_e(0)
    stage_e(1)

    for i in range(2):

        @pl.when(me + 2 * (i + 1) < n_ctx)
        def _():
            halo_copy(i).wait_send()

        mate_copy(i, lat_ref).wait_send()
    for s in range(1, n_head):
        head_copy(s).wait_send()
        headg_copy(s).wait()
    for s in range(1, PREV + 1):

        @pl.when(me >= s)
        def _():
            ctx_copy(s).wait_send()

    for p in range(PIECES):
        pair_copy(p).wait_send()
        for s in range(1, NZ):
            z_copy(p, s).wait_send()
            yz_copy(p, s).wait_send()
            yzg_copy(p, s).wait_send()
            zg_copy(p, s).wait_send()
        for s in range(1, NY):
            y_copy(p, s).wait_send()
            zy_copy(p, s).wait_send()
            zyg_copy(p, s).wait_send()
            yg_copy(p, s).wait_send()
        pairg_copy(p).wait()


def per_device(queries, latent, w_key, w_value, grad_out, segment_ids):
    n_ctx = lax.axis_size("ctx")
    n_head = lax.axis_size("head")
    vmem = pl.BlockSpec(memory_space=pltpu.VMEM)
    hbm = pl.BlockSpec(memory_space=pl.ANY)
    dma = pltpu.SemaphoreType.DMA
    rows = 80

    def buf(*shape, dtype=BF):
        return pltpu.VMEM(shape, dtype)

    def sems(*shape):
        return [dma(shape), dma(shape)]

    attn_out, grad_queries, grad_latent, grad_w = pl.pallas_call(
        functools.partial(kernel, n_ctx, n_head),
        out_shape=[
            jax.ShapeDtypeStruct((TOK, HEADS * VDIM), BF),
            jax.ShapeDtypeStruct((TOK, HEADS * QK), BF),
            jax.ShapeDtypeStruct((rows * n_head, TOK), BF),
            jax.ShapeDtypeStruct((2, LAT, HEADS * NOPE), BF),
        ],
        in_specs=[hbm, vmem, hbm, hbm, hbm, vmem],
        out_specs=[vmem] * 4,
        scratch_shapes=[
            buf(TOK, HEADS * QK),
            buf(LAT, 2 * HEADS * NOPE),
            buf(TOK, HEADS * VDIM),
            buf(LAT + ROPE, WIN),
            buf(2 * HEADS * NOPE, LAT),
            buf(HEADS, TOK, QK),
            buf(HEADS, QK, TOK),
            buf(HEADS, VDIM, TOK),
            buf(HEADS, QK, WIN),
            buf(HEADS, VDIM, WIN),
            buf(TOK, WIN, dtype=jnp.float32),
            buf(2 * HEADS * NOPE, WIN),
            buf(ROPE, WIN, dtype=jnp.float32),
            buf(PIECES, 2, LAT, COLS),
            buf(PIECES, LAT, COLS),
            buf(PIECES, LAT, COLS),
            buf(PIECES, NZ - 1, 32, COLS),
            buf(PIECES, NY - 1, 64, COLS),
            buf(PIECES, NY - 1, 16, 128),
            buf(PIECES, NZ - 1, 16, 128),
            buf(PIECES, 32, COLS),
            buf(PIECES, 64, COLS),
            buf(rows * n_head, WIN),
            buf(n_head - 1, rows, WIN),
            buf(rows, WIN),
            buf(PREV, rows, TOK),
            dma((2 + 2 * PIECES,)),
            *sems(2),
            *sems(2),
            *sems(PIECES),
            *sems(PIECES, NZ - 1),
            *sems(PIECES, NY - 1),
            *sems(PIECES, NY - 1),
            *sems(PIECES, NZ - 1),
            *sems(PIECES, NY - 1),
            *sems(PIECES, NZ - 1),
            *sems(PIECES, NZ - 1),
            *sems(PIECES, NY - 1),
            *sems(PIECES),
            *sems(n_head - 1),
            *sems(PREV),
            *sems(n_head - 1),
        ],
        compiler_params=pltpu.CompilerParams(
            collective_id=0, has_side_effects=True, vmem_limit_bytes=48 * 2**20
        ),
        name="attention",
    )(queries, latent.T, w_key, w_value, grad_out, segment_ids.reshape(n_ctx, TOK))
    return (attn_out, grad_queries, grad_latent[: LAT + ROPE].T, grad_w[0], grad_w[1])


def solution(mesh):
    return jax.shard_map(
        per_device,
        mesh=mesh,
        in_specs=(
            P("ctx", "head"),
            P("ctx", None),
            P(None, "head"),
            P(None, "head"),
            P("ctx", "head"),
            P(),
        ),
        out_specs=(
            P("ctx", "head"),
            P("ctx", "head"),
            P("ctx", None),
            P(None, "head"),
            P(None, "head"),
        ),
        check_vma=False,
    )
```

time: 472 us -> 80.3 us (0.17)
  the two profiles are of different devices: /device:TPU:32 before, /device:TPU:1 now
where the time goes in v2:
time: 80.3 us; the launch traced here: 79.9 us
  Pallas kernels  70.7 us (88%)
  local copies, waits for them, and re-layouts  8.61 us (11%)
    pallas_call x1, Pallas kernels, per_device(): pl.pallas_call(functools.partial(kernel, n_ctx, n_head), out_shape=[jax.S...  70.7 us
    unnamed x14, local copies, waits for them, and re-layouts  6.9 us

profile of v2, /device:TPU:1, one launch (start us, length us, event | category | flops | bytes accessed | tf_op | source)
XLA Modules:
  0.0 79.9 jit_solution(10491918071635152667)
XLA Ops:
  0.6 0.0 copy-start
  0.6 1.0 %copy-done = bf16[512,512]{1,0:T(8,128)(2,1)S(1)} copy-done((bf16[512,512]{1,0:T(8,128)(2,1)S(1)}, bf16[512,512]{1,0:T(8,128)(2,1)}, u32[]{:S(2)}) %copy-start) | copy-done | bytes 524312
  1.7 0.0 copy-start.1
  1.7 1.0 %copy-done.1 = bf16[512,512]{1,0:T(8,128)(2,1)S(1)} copy-done((bf16[512,512]{1,0:T(8,128)(2,1)S(1)}, bf16[512,512]{1,0:T(8,128)(2,1)}, u32[]{:S(2)}) %copy-start.1) | copy-done | bytes 524312
  2.7 0.0 copy-start.2
  2.7 0.9 %copy-done.2 = bf16[128,768]{1,0:T(8,128)(2,1)S(1)} copy-done((bf16[128,768]{1,0:T(8,128)(2,1)S(1)}, bf16[128,768]{1,0:T(8,128)(2,1)}, u32[]{:S(2)}) %copy-start.2) | copy-done | bytes 196632
  3.6 0.0 copy-start.3
  3.6 0.9 %copy-done.3 = bf16[128,576]{0,1:T(8,128)(2,1)S(1)} copy-done((bf16[128,576]{0,1:T(8,128)(2,1)S(1)}, bf16[128,576]{0,1:T(8,128)(2,1)}, u32[]{:S(2)}) %copy-start.3) | copy-done | bytes 147480
  4.6 0.0 copy-start.4
  4.6 0.9 %copy-done.4 = bf16[128,512]{1,0:T(8,128)(2,1)S(1)} copy-done((bf16[128,512]{1,0:T(8,128)(2,1)S(1)}, bf16[128,512]{1,0:T(8,128)(2,1)}, u32[]{:S(2)}) %copy-start.4) | copy-done | bytes 131096
  5.5 0.0 copy-start.5
  5.5 0.8 copy-done.5
  6.2 70.7 %attention.1 = (bf16[128,512]{1,0:T(8,128)(2,1)S(1)}, bf16[128,768]{1,0:T(8,128)(2,1)S(1)}, bf16[640,128]{1,0:T(8,128)(2,1)S(1)}, bf16[2,512,512]{2,1,0:T(8,128)(2,1)S(1)}) custom-call(bf16[128,768]{1,0:T(8,128)(2,1)S(1)} %copy-done.2, bf16[576,128]{1,0:T(8,128)(2,1)S(1)} %bitcast.8, bf16[512,512]{1,0:T(8,128)(2,1)S(1)} %copy-done, ...), custom_call_target="tpu_custom_call" | custom-call | tf_op jit(solution)/shard_map/attention/pallas_call | solution.py:527
  76.9 0.7 slice_bitcast_fusion.2
  77.5 1.0 %slice_bitcast_fusion = (bf16[512,512]{1,0:T(8,128)(2,1)}, bf16[512,512]{1,0:T(8,128)(2,1)}) fusion(bf16[2,512,512]{2,1,0:T(8,128)(2,1)S(1)} %get-tuple-element.12), kind=kLoop, calls=%fused_computation | loop fusion | bytes 2097152 | tf_op jit(solution)/shard_map/squeeze | solution.py:586
  78.6 0.7 copy.13
  79.2 0.7 copy.14
Async XLA Ops:
  0.6 1.0 %copy-start = (bf16[512,512]{1,0:T(8,128)(2,1)S(1)}, bf16[512,512]{1,0:T(8,128)(2,1)}, u32[]{:S(2)}) copy-start(bf16[512,512]{1,0:T(8,128)(2,1)} %refs_2_.1) | copy-start | bytes 1572868
  1.7 1.0 %copy-start.1 = (bf16[512,512]{1,0:T(8,128)(2,1)S(1)}, bf16[512,512]{1,0:T(8,128)(2,1)}, u32[]{:S(2)}) copy-start(bf16[512,512]{1,0:T(8,128)(2,1)} %refs_3_.1) | copy-start | bytes 1572868
  2.7 0.9 %copy-start.2 = (bf16[128,768]{1,0:T(8,128)(2,1)S(1)}, bf16[128,768]{1,0:T(8,128)(2,1)}, u32[]{:S(2)}) copy-start(bf16[128,768]{1,0:T(8,128)(2,1)} %refs_0_.1) | copy-start | bytes 589828
  3.6 0.9 %copy-start.3 = (bf16[128,576]{0,1:T(8,128)(2,1)S(1)}, bf16[128,576]{0,1:T(8,128)(2,1)}, u32[]{:S(2)}) copy-start(bf16[128,576]{0,1:T(8,128)(2,1)} %param.7) | copy-start | bytes 442372
  4.6 0.9 %copy-start.4 = (bf16[128,512]{1,0:T(8,128)(2,1)S(1)}, bf16[128,512]{1,0:T(8,128)(2,1)}, u32[]{:S(2)}) copy-start(bf16[128,512]{1,0:T(8,128)(2,1)} %refs_4_.1) | copy-start | bytes 393220
  5.5 0.8 copy-start.5

commit v3 on v2

--- a/solution.py
+++ b/solution.py
@@ -49,11 +49,11 @@
 def kernel(n_ctx, n_head, *refs):
     (
         q_hbm,
-        lat_ref,
+        lat_hbm,
         wk_hbm,
         wv_hbm,
         do_hbm,
-        seg_ref,
+        seg_hbm,
         attn_ref,
         gq_ref,
         gl_out,
@@ -61,6 +61,7 @@
         q_ref,
         wcat,
         do_ref,
+        seg_ref,
         win,
         wt,
         qs,
@@ -81,12 +82,16 @@
         z_part,
         y_part,
         glb,
-        head_in,
+        x_in,
+        x_part,
+        yl_in,
         ctx_part,
         ctx_in,
         load_sem,
         halo_s,
         halo_r,
+        far_s,
+        far_r,
         mate_s,
         mate_r,
         pair_s,
@@ -109,8 +114,10 @@
         yg_r,
         pairg_s,
         pairg_r,
-        head_s,
-        head_r,
+        x_s,
+        x_r,
+        yl_s,
+        yl_r,
         ctx_s,
         ctx_r,
         headg_s,
@@ -123,6 +130,9 @@
     y = me // (2 * NZ)
     partner = me + 1 - 2 * core
     rows = glb.shape[0] // n_head
+    x = head // 2
+    y_lo = lax.rem(head, 2)
+    head_rows = pl.ds(mult(head * rows, 16), rows)
 
     def z_dev(s):
         return {"ctx": (y * NZ + lax.rem(z + s, NZ)) * 2 + core}
@@ -138,10 +148,14 @@
             src_ref=src, dst_ref=dst, send_sem=send, recv_sem=recv, device_id=device, device_id_type=MESH
         )
 
+    pad = pl.ds(LAT + ROPE, win.shape[0] - LAT - ROPE)
+    win[pad, slot_cols(PREV)] = jnp.zeros((win.shape[0] - LAT - ROPE, TOK), BF)
+    live = pl.ds(0, LAT + ROPE)
+    own_block = win.at[live, slot_cols(PREV)]
     loads = [
         pltpu.make_async_copy(src, dst, load_sem.at[i])
         for i, (src, dst) in enumerate(
-            [(q_hbm, q_ref), (do_hbm, do_ref)]
+            [(lat_hbm, own_block), (seg_hbm, seg_ref), (q_hbm, q_ref), (do_hbm, do_ref)]
             + [
                 (w.at[:, pl.ds(p * COLS, COLS)], wcat.at[:, pl.ds((2 * p + kind) * COLS, COLS)])
                 for p in range(PIECES)
@@ -179,29 +193,45 @@
         NZ - 1 + NY - 1 + n_head + jnp.minimum(me, PREV) + jnp.minimum(n_ctx - 1 - me, PREV),
     )
 
-    def halo_copy(i):
-        d = 2 * (i + 1)
-        return remote(
-            lat_ref, win.at[:, slot_cols(PREV - d)], halo_s.at[i], halo_r.at[i], {"ctx": me + d}
-        )
+    near = remote(
+        own_block, win.at[live, slot_cols(2)], halo_s.at[0], halo_r.at[0], {"ctx": me + 2}
+    )
+    far = remote(
+        win.at[head_rows, slot_cols(PREV)],
+        win.at[head_rows, slot_cols(0)],
+        halo_s.at[1],
+        halo_r.at[1],
+        {"ctx": me + 4},
+    )
+
+    def far_copy(s):
+        block = win.at[head_rows, slot_cols(0)]
+        return remote(block, block, far_s.at[s - 1], far_r.at[s - 1], {"head": at_head(s)})
 
     def mate_copy(i, src):
         return remote(
-            src, win.at[:, slot_cols(PREV - 1 - 2 * i)], mate_s.at[i], mate_r.at[i], {"ctx": partner}
+            win.at[live, slot_cols(src)],
+            win.at[live, slot_cols(PREV - 1 - 2 * i)],
+            mate_s.at[i],
+            mate_r.at[i],
+            {"ctx": partner},
         )
 
-    for i in range(2):
-
-        @pl.when(me + 2 * (i + 1) < n_ctx)
-        def _():
-            halo_copy(i).start()
+    loads[0].wait()
+
+    @pl.when(me + 4 < n_ctx)
+    def _():
+        far.start()
+
+    @pl.when(me + 2 < n_ctx)
+    def _():
+        near.start()
 
     @pl.when(core == 0)
     def _():
-        mate_copy(0, lat_ref).start()
-
-    win[:, slot_cols(PREV)] = lat_ref[...]
-    for load in loads:
+        mate_copy(0, PREV).start()
+
+    for load in loads[1:]:
         load.wait()
     for i in range(2 * PIECES):
         wt[pl.ds(i * COLS, COLS), :] = wcat[:, pl.ds(i * COLS, COLS)].T
@@ -224,45 +254,57 @@
 
     def project(start, size):
         cols = pl.ds(start, size)
+        each = HEADS // PIECES
+        for p in range(PIECES):
+            made = nn(wt[pl.ds(2 * p * COLS, 2 * COLS), :], win[pl.ds(0, LAT), cols]).astype(BF)
+            for j in range(each):
+                kt[p * each + j, pl.ds(0, NOPE), cols] = made[j * NOPE : (j + 1) * NOPE]
+                vt[p * each + j, :, cols] = made[COLS + j * VDIM : COLS + (j + 1) * VDIM]
         for h in range(HEADS):
-            p, j = divmod(h, HEADS // PIECES)
-            base = 2 * p * COLS + j * NOPE
-            kt[h, pl.ds(0, NOPE), cols] = nn(wt[pl.ds(base, NOPE), :], win[pl.ds(0, LAT), cols]).astype(BF)
             kt[h, pl.ds(NOPE, ROPE), cols] = win[pl.ds(LAT, ROPE), cols]
-            vt[h, :, cols] = nn(wt[pl.ds(base + COLS, NOPE), :], win[pl.ds(0, LAT), cols]).astype(BF)
 
     project(PREV * TOK, TOK)
 
-    def arrived(i):
-        d = 2 * (i + 1)
-
-        @pl.when(me >= d)
-        def _():
-            halo_copy(i).wait_recv()
-
-        @pl.when(me < d)
-        def _():
-            win[:, slot_cols(PREV - d)] = jnp.zeros((LAT + ROPE, TOK), BF)
-
-    arrived(0)
+    @pl.when(me >= 4)
+    def _():
+        far.wait_recv()
+        for s in range(1, n_head):
+            far_copy(s).start()
+
+    @pl.when(me >= 2)
+    def _():
+        near.wait_recv()
+
+    @pl.when(me < 2)
+    def _():
+        win[live, slot_cols(2)] = jnp.zeros((LAT + ROPE, TOK), BF)
 
     @pl.when(core == 0)
     def _():
-        mate_copy(1, win.at[:, slot_cols(2)]).start()
+        mate_copy(1, 2).start()
 
     @pl.when(core == 1)
     def _():
-        mate_copy(0, win.at[:, slot_cols(2)]).start()
-
-    arrived(1)
+        mate_copy(0, 2).start()
+
+    mate_copy(0, PREV).wait_recv()
+    project(2 * TOK, 2 * TOK)
+
+    @pl.when(me >= 4)
+    def _():
+        for s in range(1, n_head):
+            far_copy(s).wait_recv()
+
+    @pl.when(me < 4)
+    def _():
+        win[live, slot_cols(0)] = jnp.zeros((LAT + ROPE, TOK), BF)
 
     @pl.when(core == 1)
     def _():
-        mate_copy(1, win.at[:, slot_cols(0)]).start()
-
-    for i in range(2):
-        mate_copy(i, lat_ref).wait_recv()
-    project(0, PREV * TOK)
+        mate_copy(1, 0).start()
+
+    mate_copy(1, PREV).wait_recv()
+    project(0, 2 * TOK)
 
     def one_head(h):
         p, j = divmod(h, HEADS // PIECES)
@@ -401,10 +443,23 @@
             yg_copy(p, s).wait_recv()
         pairg_copy(p).start()
 
-    def head_copy(s):
-        block = pl.ds(mult(at_head(s) * rows, 16), rows)
+    def x_copy(s):
+        there = lax.rem(x + s, n_head // 2)
         return remote(
-            glb.at[block], head_in.at[s - 1], head_s.at[s - 1], head_r.at[s - 1], {"head": at_head(s)}
+            glb.at[pl.ds(mult(there * 2 * rows, 16), 2 * rows)],
+            x_in.at[s - 1],
+            x_s.at[s - 1],
+            x_r.at[s - 1],
+            {"head": there * 2 + y_lo},
+        )
+
+    def yl_copy():
+        return remote(
+            x_part.at[pl.ds(mult((1 - y_lo) * rows, 16), rows)],
+            yl_in,
+            yl_s,
+            yl_r,
+            {"head": head + 1 - 2 * y_lo},
         )
 
     def ctx_copy(s):
@@ -417,7 +472,7 @@
         )
 
     def headg_copy(s):
-        block = gl_out.at[pl.ds(mult(head * rows, 16), rows)]
+        block = gl_out.at[head_rows]
         return remote(block, block, headg_s.at[s - 1], headg_r.at[s - 1], {"head": at_head(s)})
 
     def latent_terms():
@@ -426,14 +481,20 @@
         glb[pl.ds(LAT + ROPE, glb.shape[0] - LAT - ROPE), :] = jnp.zeros(
             (glb.shape[0] - LAT - ROPE, WIN), BF
         )
-        for s in range(1, n_head):
-            head_copy(s).start()
-
-    def latent_heads():
-        total = f32(glb[pl.ds(mult(head * rows, 16), rows), :])
-        for s in range(1, n_head):
-            head_copy(s).wait_recv()
-            total += f32(head_in[s - 1])
+        for s in range(1, n_head // 2):
+            x_copy(s).start()
+
+    def latent_x():
+        total = f32(glb[pl.ds(mult(x * 2 * rows, 16), 2 * rows), :])
+        for s in range(1, n_head // 2):
+            x_copy(s).wait_recv()
+            total += f32(x_in[s - 1])
+        x_part[...] = total.astype(BF)
+        yl_copy().start()
+
+    def latent_y():
+        yl_copy().wait_recv()
+        total = f32(x_part[pl.ds(mult(y_lo * rows, 16), rows), :]) + f32(yl_in[...])
         ctx_part[...] = total.astype(BF)
         for s in range(1, PREV + 1):
 
@@ -455,7 +516,7 @@
         total = f32(ctx_part[:, slot_cols(PREV)])
         for s in range(1, PREV + 1):
             total += f32(ctx_in[s - 1])
-        gl_out[pl.ds(mult(head * rows, 16), rows), :] = total.astype(BF)
+        gl_out[head_rows, :] = total.astype(BF)
         for s in range(1, n_head):
             headg_copy(s).start()
 
@@ -465,29 +526,41 @@
     one_head(2)
     stage_a(0)
     one_head(3)
+    latent_terms()
     weight_terms(1)
-    latent_terms()
     stage_a(1)
     stage_b(0)
-    latent_heads()
     stage_b(1)
     stage_c(0)
-    latent_blocks()
+    latent_x()
     stage_c(1)
     stage_d(0)
+    latent_y()
     stage_d(1)
+    latent_blocks()
     stage_e(0)
     stage_e(1)
 
+    @pl.when(me + 4 < n_ctx)
+    def _():
+        far.wait_send()
+
+    @pl.when(me + 2 < n_ctx)
+    def _():
+        near.wait_send()
+
     for i in range(2):
-
-        @pl.when(me + 2 * (i + 1) < n_ctx)
-        def _():
-            halo_copy(i).wait_send()
-
-        mate_copy(i, lat_ref).wait_send()
+        mate_copy(i, PREV).wait_send()
+
+    @pl.when(me >= 4)
+    def _():
+        for s in range(1, n_head):
+            far_copy(s).wait_send()
+
+    for s in range(1, n_head // 2):
+        x_copy(s).wait_send()
+    yl_copy().wait_send()
     for s in range(1, n_head):
-        head_copy(s).wait_send()
         headg_copy(s).wait()
     for s in range(1, PREV + 1):
 
@@ -510,11 +583,37 @@
         pairg_copy(p).wait()
 
 
+def write_out(attn, gq, gl, gw, attn_out, gq_out, gl_out, gk_out, gv_out, *rest):
+    stages, load_sem, store_sem = rest[:5], rest[5], rest[6]
+    pairs = [
+        (gw.at[0], gk_out),
+        (gw.at[1], gv_out),
+        (gq, gq_out),
+        (gl.at[pl.ds(0, LAT + ROPE)], gl_out),
+        (attn, attn_out),
+    ]
+    loads = [
+        pltpu.make_async_copy(src, stage, load_sem.at[i])
+        for i, ((src, _), stage) in enumerate(zip(pairs, stages))
+    ]
+    stores = [
+        pltpu.make_async_copy(stage, dst, store_sem.at[i])
+        for i, ((_, dst), stage) in enumerate(zip(pairs, stages))
+    ]
+    for load in loads:
+        load.start()
+    for load, store in zip(loads, stores):
+        load.wait()
+        store.start()
+    for store in stores:
+        store.wait()
+
+
 def per_device(queries, latent, w_key, w_value, grad_out, segment_ids):
     n_ctx = lax.axis_size("ctx")
     n_head = lax.axis_size("head")
     vmem = pl.BlockSpec(memory_space=pltpu.VMEM)
-    hbm = pl.BlockSpec(memory_space=pl.ANY)
+    hbm = pl.BlockSpec(memory_space=pltpu.HBM)
     dma = pltpu.SemaphoreType.DMA
     rows = 80
 
@@ -532,13 +631,14 @@
             jax.ShapeDtypeStruct((rows * n_head, TOK), BF),
             jax.ShapeDtypeStruct((2, LAT, HEADS * NOPE), BF),
         ],
-        in_specs=[hbm, vmem, hbm, hbm, hbm, vmem],
+        in_specs=[hbm] * 6,
         out_specs=[vmem] * 4,
         scratch_shapes=[
             buf(TOK, HEADS * QK),
             buf(LAT, 2 * HEADS * NOPE),
             buf(TOK, HEADS * VDIM),
-            buf(LAT + ROPE, WIN),
+            buf(n_ctx, TOK, dtype=jnp.int32),
+            buf(rows * n_head, WIN),
             buf(2 * HEADS * NOPE, LAT),
             buf(HEADS, TOK, QK),
             buf(HEADS, QK, TOK),
@@ -558,11 +658,14 @@
             buf(PIECES, 32, COLS),
             buf(PIECES, 64, COLS),
             buf(rows * n_head, WIN),
-            buf(n_head - 1, rows, WIN),
+            buf(n_head // 2 - 1, 2 * rows, WIN),
+            buf(2 * rows, WIN),
+            buf(rows, WIN),
             buf(rows, WIN),
             buf(PREV, rows, TOK),
-            dma((2 + 2 * PIECES,)),
+            dma((4 + 2 * PIECES,)),
             *sems(2),
+            *sems(n_head - 1),
             *sems(2),
             *sems(PIECES),
             *sems(PIECES, NZ - 1),
@@ -574,16 +677,41 @@
             *sems(PIECES, NZ - 1),
             *sems(PIECES, NY - 1),
             *sems(PIECES),
-            *sems(n_head - 1),
+            *sems(n_head // 2 - 1),
+            dma,
+            dma,
             *sems(PREV),
             *sems(n_head - 1),
         ],
         compiler_params=pltpu.CompilerParams(
-            collective_id=0, has_side_effects=True, vmem_limit_bytes=48 * 2**20
+            collective_id=0, has_side_effects=True, vmem_limit_bytes=60 * 2**20
         ),
         name="attention",
     )(queries, latent.T, w_key, w_value, grad_out, segment_ids.reshape(n_ctx, TOK))
-    return (attn_out, grad_queries, grad_latent[: LAT + ROPE].T, grad_w[0], grad_w[1])
+    any_space = pl.BlockSpec(memory_space=pl.ANY)
+    attn_out, grad_queries, grad_latent, grad_w_key, grad_w_value = pl.pallas_call(
+        write_out,
+        out_shape=[
+            jax.ShapeDtypeStruct((TOK, HEADS * VDIM), BF),
+            jax.ShapeDtypeStruct((TOK, HEADS * QK), BF),
+            jax.ShapeDtypeStruct((LAT + ROPE, TOK), BF),
+            jax.ShapeDtypeStruct((LAT, HEADS * NOPE), BF),
+            jax.ShapeDtypeStruct((LAT, HEADS * NOPE), BF),
+        ],
+        in_specs=[any_space] * 4,
+        out_specs=[hbm] * 5,
+        scratch_shapes=[
+            buf(LAT, HEADS * NOPE),
+            buf(LAT, HEADS * NOPE),
+            buf(TOK, HEADS * QK),
+            buf(LAT + ROPE, TOK),
+            buf(TOK, HEADS * VDIM),
+            *sems(5),
+        ],
+        compiler_params=pltpu.CompilerParams(vmem_limit_bytes=60 * 2**20),
+        name="write_out",
+    )(attn_out, grad_queries, grad_latent, grad_w)
+    return (attn_out, grad_queries, grad_latent.T, grad_w_key, grad_w_value)
 
 
 def solution(mesh):

time: 80.3 us -> 65.5 us (0.82)
  local copies, waits for them, and re-layouts: 8.61 us -> 0 us
  Pallas kernels: 70.7 us -> 64.7 us
    pallas_call x1, Pallas kernels: 70.7 us -> 62.5 us  [per_device(): pl.pallas_call(functools.partial(kernel, n_ctx, n_head), out_shape=[jax.S...]
    unnamed x14 -> x0, local copies, waits for them, and re-layouts: 6.9 us -> none
    pallas_call x0 -> x1, Pallas kernels: none -> 2.24 us  [per_device(): pl.pallas_call(write_out, out_shape=[jax.ShapeDtypeStruct((TOK, HEADS * V...]
    squeeze x1 -> x0, local copies, waits for them, and re-layouts: 1.03 us -> none  [per_device(): grad_w[1]]
where the time goes in v3:
time: 65.5 us; the launch traced here: 65.4 us
  Pallas kernels  64.7 us (99%)
    pallas_call x1, Pallas kernels, per_device(): pl.pallas_call(functools.partial(kernel, n_ctx, n_head), out_shape=[jax.S...  62.5 us
    pallas_call x1, Pallas kernels, per_device(): pl.pallas_call(write_out, out_shape=[jax.ShapeDtypeStruct((TOK, HEADS * V...  2.24 us

profile of v3, /device:TPU:1, one launch (start us, length us, event | category | flops | bytes accessed | tf_op | source)
XLA Modules:
  0.0 65.4 jit_solution(7960607014037420027)
XLA Ops:
  0.6 62.5 %attention.1 = (bf16[128,512]{1,0:T(8,128)(2,1)}, bf16[128,768]{1,0:T(8,128)(2,1)}, bf16[640,128]{1,0:T(8,128)(2,1)}, bf16[2,512,512]{2,1,0:T(8,128)(2,1)}) custom-call(bf16[128,768]{1,0:T(8,128)(2,1)} %refs_0_.1, bf16[576,128]{1,0:T(8,128)(2,1)} %bitcast.3, bf16[512,512]{1,0:T(8,128)(2,1)} %refs_2_.1, bf16[512,512]{1,0:T(8,128)(2,1)} %refs_3_.1, ...), custom_call_target="tpu_custom_call" | custom-call | tf_op jit(solution)/shard_map/attention/pallas_call | solution.py:626
  63.1 2.2 %write_out.1 = (bf16[128,512]{1,0:T(8,128)(2,1)}, bf16[128,768]{1,0:T(8,128)(2,1)}, bf16[576,128]{1,0:T(8,128)(2,1)}, bf16[512,512]{1,0:T(8,128)(2,1)}, bf16[512,512]{1,0:T(8,128)(2,1)}) custom-call(bf16[128,512]{1,0:T(8,128)(2,1)} %get-tuple-element.14.attn, bf16[128,768]{1,0:T(8,128)(2,1)} %get-tuple-element.15.gq, bf16[640,128]{1,0:T(8,128)(2,1)} %get-tuple-element.16.gl, ...), custom_call_target="tpu_custom_call" | custom-call | tf_op jit(solution)/shard_map/write_out/pallas_call | solution.py:692

commit v4 on v3

--- a/solution.py
+++ b/solution.py
@@ -148,6 +148,9 @@
             src_ref=src, dst_ref=dst, send_sem=send, recv_sem=recv, device_id=device, device_id_type=MESH
         )
 
+    def phase(block, send, recv):
+        return remote(block, block, send, recv, {"ctx": partner})
+
     pad = pl.ds(LAT + ROPE, win.shape[0] - LAT - ROPE)
     win[pad, slot_cols(PREV)] = jnp.zeros((win.shape[0] - LAT - ROPE, TOK), BF)
     live = pl.ds(0, LAT + ROPE)
@@ -206,7 +209,7 @@
 
     def far_copy(s):
         block = win.at[head_rows, slot_cols(0)]
-        return remote(block, block, far_s.at[s - 1], far_r.at[s - 1], {"head": at_head(s)})
+        return remote(block, block, far_s, far_r, {"head": at_head(s)})
 
     def mate_copy(i, src):
         return remote(
@@ -231,10 +234,10 @@
     def _():
         mate_copy(0, PREV).start()
 
+    far_all = phase(win.at[pl.ds(0, (n_head - 1) * rows), slot_cols(0)], far_s, far_r)
+
     for load in loads[1:]:
         load.wait()
-    for i in range(2 * PIECES):
-        wt[pl.ds(i * COLS, COLS), :] = wcat[:, pl.ds(i * COLS, COLS)].T
     for h in range(HEADS):
         block = q_ref[:, pl.ds(h * QK, QK)]
         qs[h] = block
@@ -252,6 +255,14 @@
             )
         bias[:, slot_cols(s)] = jnp.where(allowed, 0.0, -jnp.inf)
 
+    @pl.when(me >= 4)
+    def _():
+        far.wait_recv()
+        for s in range(1, n_head):
+            far_copy(s).start()
+
+    for i in range(2 * PIECES):
+        wt[pl.ds(i * COLS, COLS), :] = wcat[:, pl.ds(i * COLS, COLS)].T
     def project(start, size):
         cols = pl.ds(start, size)
         each = HEADS // PIECES
@@ -265,12 +276,6 @@
 
     project(PREV * TOK, TOK)
 
-    @pl.when(me >= 4)
-    def _():
-        far.wait_recv()
-        for s in range(1, n_head):
-            far_copy(s).start()
-
     @pl.when(me >= 2)
     def _():
         near.wait_recv()
@@ -292,8 +297,7 @@
 
     @pl.when(me >= 4)
     def _():
-        for s in range(1, n_head):
-            far_copy(s).wait_recv()
+        far_all.wait_recv()
 
     @pl.when(me < 4)
     def _():
@@ -302,9 +306,24 @@
     @pl.when(core == 1)
     def _():
         mate_copy(1, 0).start()
+
+    @pl.when(me + 4 < n_ctx)
+    def _():
+        far.wait_send()
+
+    @pl.when(me + 2 < n_ctx)
+    def _():
+        near.wait_send()
 
     mate_copy(1, PREV).wait_recv()
     project(0, 2 * TOK)
+
+    for i in range(2):
+        mate_copy(i, PREV).wait_send()
+
+    @pl.when(me >= 4)
+    def _():
+        far_all.wait_send()
 
     def one_head(h):
         p, j = divmod(h, HEADS // PIECES)
@@ -337,22 +356,22 @@
 
     def z_copy(p, s):
         block = pl.ds(mult(lax.rem(z + s, NZ) * 32, 32), 32)
-        return remote(half.at[p, block], z_in.at[p, s - 1], z_s.at[p, s - 1], z_r.at[p, s - 1], z_dev(s))
+        return remote(half.at[p, block], z_in.at[p, s - 1], z_s.at[p], z_r.at[p], z_dev(s))
 
     def y_copy(p, s):
         block = pl.ds(mult(256 + lax.rem(y + s, NY) * 64, 64), 64)
-        return remote(half.at[p, block], y_in.at[p, s - 1], y_s.at[p, s - 1], y_r.at[p, s - 1], y_dev(s))
+        return remote(half.at[p, block], y_in.at[p, s - 1], y_s.at[p], y_r.at[p], y_dev(s))
 
     def small(i):
-        return pl.ds(mult(i // 2 * 16, 16), 16), pl.ds(mult(lax.rem(i, 2) * 128, 128), 128)
+        return pl.ds(mult(i // 2 * 16, 16), 16), pl.ds(mult(lax.rem(i, 2) * (COLS // 2), 128), COLS // 2)
 
     def zy_copy(p, s):
         r, c = small(lax.rem(y + s, NY))
-        return remote(z_part.at[p, r, c], zy_in.at[p, s - 1], zy_s.at[p, s - 1], zy_r.at[p, s - 1], y_dev(s))
+        return remote(z_part.at[p, r, c], zy_in.at[p, s - 1], zy_s.at[p], zy_r.at[p], y_dev(s))
 
     def yz_copy(p, s):
         r, c = small(lax.rem(z + s, NZ))
-        return remote(y_part.at[p, r, c], yz_in.at[p, s - 1], yz_s.at[p, s - 1], yz_r.at[p, s - 1], z_dev(s))
+        return remote(y_part.at[p, r, c], yz_in.at[p, s - 1], yz_s.at[p], yz_r.at[p], z_dev(s))
 
     def z_place(p):
         return gw_out.at[core, pl.ds(mult(z * 32, 32), 32), pl.ds(p * COLS, COLS)]
@@ -362,27 +381,51 @@
 
     def zy_place(p):
         r = pl.ds(mult(z * 32 + y // 2 * 16, 16), 16)
-        return gw_out.at[core, r, pl.ds(mult(p * COLS + lax.rem(y, 2) * 128, 128), 128)]
+        return gw_out.at[core, r, pl.ds(mult(p * COLS + lax.rem(y, 2) * (COLS // 2), 128), COLS // 2)]
 
     def yz_place(p):
         r = pl.ds(mult(256 + y * 64 + z // 2 * 16, 16), 16)
-        return gw_out.at[core, r, pl.ds(mult(p * COLS + lax.rem(z, 2) * 128, 128), 128)]
+        return gw_out.at[core, r, pl.ds(mult(p * COLS + lax.rem(z, 2) * (COLS // 2), 128), COLS // 2)]
 
     def zyg_copy(p, s):
-        return remote(zy_place(p), zy_place(p), zyg_s.at[p, s - 1], zyg_r.at[p, s - 1], y_dev(s))
+        return remote(zy_place(p), zy_place(p), zyg_s.at[p], zyg_r.at[p], y_dev(s))
 
     def yzg_copy(p, s):
-        return remote(yz_place(p), yz_place(p), yzg_s.at[p, s - 1], yzg_r.at[p, s - 1], z_dev(s))
+        return remote(yz_place(p), yz_place(p), yzg_s.at[p], yzg_r.at[p], z_dev(s))
 
     def zg_copy(p, s):
-        return remote(z_place(p), z_place(p), zg_s.at[p, s - 1], zg_r.at[p, s - 1], z_dev(s))
+        return remote(z_place(p), z_place(p), zg_s.at[p], zg_r.at[p], z_dev(s))
 
     def yg_copy(p, s):
-        return remote(y_place(p), y_place(p), yg_s.at[p, s - 1], yg_r.at[p, s - 1], y_dev(s))
+        return remote(y_place(p), y_place(p), yg_s.at[p], yg_r.at[p], y_dev(s))
 
     def pairg_copy(p):
         block = gw_out.at[core, :, pl.ds(p * COLS, COLS)]
         return remote(block, block, pairg_s.at[p], pairg_r.at[p], {"ctx": partner})
+
+    def z_phase(p):
+        return phase(z_in.at[p], z_s.at[p], z_r.at[p])
+
+    def y_phase(p):
+        return phase(y_in.at[p], y_s.at[p], y_r.at[p])
+
+    def zy_phase(p):
+        return phase(zy_in.at[p], zy_s.at[p], zy_r.at[p])
+
+    def yz_phase(p):
+        return phase(yz_in.at[p], yz_s.at[p], yz_r.at[p])
+
+    def zyg_phase(p):
+        return phase(zy_in.at[p], zyg_s.at[p], zyg_r.at[p])
+
+    def yzg_phase(p):
+        return phase(yz_in.at[p], yzg_s.at[p], yzg_r.at[p])
+
+    def zg_phase(p):
+        return phase(z_in.at[p], zg_s.at[p], zg_r.at[p])
+
+    def yg_phase(p):
+        return phase(y_in.at[p], yg_s.at[p], yg_r.at[p])
 
     def stage_a(p):
         pair_copy(p).wait_recv()
@@ -391,65 +434,70 @@
             z_copy(p, s).start()
         for s in range(1, NY):
             y_copy(p, s).start()
+        pair_copy(p).wait_send()
 
     def stage_b(p):
+        z_phase(p).wait_recv()
         total = f32(half[p, pl.ds(mult(z * 32, 32), 32), :])
         for s in range(1, NZ):
-            z_copy(p, s).wait_recv()
             total += f32(z_in[p, s - 1])
         z_part[p] = total.astype(BF)
         for s in range(1, NY):
             zy_copy(p, s).start()
+        y_phase(p).wait_recv()
         total = f32(half[p, pl.ds(mult(256 + y * 64, 64), 64), :])
         for s in range(1, NY):
-            y_copy(p, s).wait_recv()
             total += f32(y_in[p, s - 1])
         y_part[p] = total.astype(BF)
         for s in range(1, NZ):
             yz_copy(p, s).start()
+        z_phase(p).wait_send()
+        y_phase(p).wait_send()
 
     def stage_c(p):
+        zy_phase(p).wait_recv()
         r, c = small(y)
         total = f32(z_part[p, r, c])
         for s in range(1, NY):
-            zy_copy(p, s).wait_recv()
             total += f32(zy_in[p, s - 1])
         zy_place(p)[...] = total.astype(BF)
         for s in range(1, NY):
             zyg_copy(p, s).start()
+        yz_phase(p).wait_recv()
         r, c = small(z)
         total = f32(y_part[p, r, c])
         for s in range(1, NZ):
-            yz_copy(p, s).wait_recv()
             total += f32(yz_in[p, s - 1])
         yz_place(p)[...] = total.astype(BF)
         for s in range(1, NZ):
             yzg_copy(p, s).start()
+        zy_phase(p).wait_send()
+        yz_phase(p).wait_send()
 
     def stage_d(p):
-        for s in range(1, NY):
-            zyg_copy(p, s).wait_recv()
+        zyg_phase(p).wait_recv()
         for s in range(1, NZ):
             zg_copy(p, s).start()
-        for s in range(1, NZ):
-            yzg_copy(p, s).wait_recv()
+        yzg_phase(p).wait_recv()
         for s in range(1, NY):
             yg_copy(p, s).start()
+        zyg_phase(p).wait_send()
+        yzg_phase(p).wait_send()
 
     def stage_e(p):
-        for s in range(1, NZ):
-            zg_copy(p, s).wait_recv()
-        for s in range(1, NY):
-            yg_copy(p, s).wait_recv()
+        zg_phase(p).wait_recv()
+        yg_phase(p).wait_recv()
         pairg_copy(p).start()
+        zg_phase(p).wait_send()
+        yg_phase(p).wait_send()
 
     def x_copy(s):
         there = lax.rem(x + s, n_head // 2)
         return remote(
             glb.at[pl.ds(mult(there * 2 * rows, 16), 2 * rows)],
             x_in.at[s - 1],
-            x_s.at[s - 1],
-            x_r.at[s - 1],
+            x_s,
+            x_r,
             {"head": there * 2 + y_lo},
         )
 
@@ -473,7 +521,7 @@
 
     def headg_copy(s):
         block = gl_out.at[head_rows]
-        return remote(block, block, headg_s.at[s - 1], headg_r.at[s - 1], {"head": at_head(s)})
+        return remote(block, block, headg_s, headg_r, {"head": at_head(s)})
 
     def latent_terms():
         glb[pl.ds(0, LAT), :] = nn(wcat[...], dcat[...]).astype(BF)
@@ -485,12 +533,13 @@
             x_copy(s).start()
 
     def latent_x():
+        phase(x_in, x_s, x_r).wait_recv()
         total = f32(glb[pl.ds(mult(x * 2 * rows, 16), 2 * rows), :])
         for s in range(1, n_head // 2):
-            x_copy(s).wait_recv()
             total += f32(x_in[s - 1])
         x_part[...] = total.astype(BF)
         yl_copy().start()
+        phase(x_in, x_s, x_r).wait_send()
 
     def latent_y():
         yl_copy().wait_recv()
@@ -501,6 +550,8 @@
             @pl.when(me >= s)
             def _():
                 ctx_copy(s).start()
+
+        yl_copy().wait_send()
 
     def latent_blocks():
         for s in range(1, PREV + 1):
@@ -526,60 +577,29 @@
     one_head(2)
     stage_a(0)
     one_head(3)
+    weight_terms(1)
     latent_terms()
-    weight_terms(1)
     stage_a(1)
     stage_b(0)
     stage_b(1)
     stage_c(0)
+    stage_c(1)
     latent_x()
-    stage_c(1)
     stage_d(0)
+    stage_d(1)
     latent_y()
-    stage_d(1)
+    stage_e(0)
     latent_blocks()
-    stage_e(0)
     stage_e(1)
 
-    @pl.when(me + 4 < n_ctx)
-    def _():
-        far.wait_send()
-
-    @pl.when(me + 2 < n_ctx)
-    def _():
-        near.wait_send()
-
-    for i in range(2):
-        mate_copy(i, PREV).wait_send()
-
-    @pl.when(me >= 4)
-    def _():
-        for s in range(1, n_head):
-            far_copy(s).wait_send()
-
-    for s in range(1, n_head // 2):
-        x_copy(s).wait_send()
-    yl_copy().wait_send()
-    for s in range(1, n_head):
-        headg_copy(s).wait()
     for s in range(1, PREV + 1):
 
         @pl.when(me >= s)
         def _():
             ctx_copy(s).wait_send()
 
+    phase(gl_out.at[pl.ds(0, (n_head - 1) * rows)], headg_s, headg_r).wait()
     for p in range(PIECES):
-        pair_copy(p).wait_send()
-        for s in range(1, NZ):
-            z_copy(p, s).wait_send()
-            yz_copy(p, s).wait_send()
-            yzg_copy(p, s).wait_send()
-            zg_copy(p, s).wait_send()
-        for s in range(1, NY):
-            y_copy(p, s).wait_send()
-            zy_copy(p, s).wait_send()
-            zyg_copy(p, s).wait_send()
-            yg_copy(p, s).wait_send()
         pairg_copy(p).wait()
 
 
@@ -653,8 +673,8 @@
             buf(PIECES, LAT, COLS),
             buf(PIECES, NZ - 1, 32, COLS),
             buf(PIECES, NY - 1, 64, COLS),
-            buf(PIECES, NY - 1, 16, 128),
-            buf(PIECES, NZ - 1, 16, 128),
+            buf(PIECES, NY - 1, 16, COLS // 2),
+            buf(PIECES, NZ - 1, 16, COLS // 2),
             buf(PIECES, 32, COLS),
             buf(PIECES, 64, COLS),
             buf(rows * n_head, WIN),
@@ -665,23 +685,26 @@
             buf(PREV, rows, TOK),
             dma((4 + 2 * PIECES,)),
             *sems(2),
-            *sems(n_head - 1),
+            dma,
+            dma,
             *sems(2),
             *sems(PIECES),
-            *sems(PIECES, NZ - 1),
-            *sems(PIECES, NY - 1),
-            *sems(PIECES, NY - 1),
-            *sems(PIECES, NZ - 1),
-            *sems(PIECES, NY - 1),
-            *sems(PIECES, NZ - 1),
-            *sems(PIECES, NZ - 1),
-            *sems(PIECES, NY - 1),
-            *sems(PIECES),
-            *sems(n_head // 2 - 1),
+            *sems(PIECES),
+            *sems(PIECES),
+            *sems(PIECES),
+            *sems(PIECES),
+            *sems(PIECES),
+            *sems(PIECES),
+            *sems(PIECES),
+            *sems(PIECES),
+            *sems(PIECES),
+            dma,
+            dma,
             dma,
             dma,
             *sems(PREV),
-            *sems(n_head - 1),
+            dma,
+            dma,
         ],
         compiler_params=pltpu.CompilerParams(
             collective_id=0, has_side_effects=True, vmem_limit_bytes=60 * 2**20

time: 65.5 us -> 63 us (0.962); the launches traced: 65.4 us -> 62.2 us
  Pallas kernels: 64.7 us -> 61.5 us
    pallas_call x1, Pallas kernels: 62.5 us -> 59.3 us  [per_device(): pl.pallas_call(functools.partial(kernel, n_ctx, n_head), out_shape=[jax.S...]
where the time goes in v4:
time: 63 us; the launch traced here: 62.2 us
  Pallas kernels  61.5 us (98%)
  between operations  0.64 us (1%)
    pallas_call x1, Pallas kernels, per_device(): pl.pallas_call(functools.partial(kernel, n_ctx, n_head), out_shape=[jax.S...  59.3 us
    pallas_call x1, Pallas kernels, per_device(): pl.pallas_call(write_out, out_shape=[jax.ShapeDtypeStruct((TOK, HEADS * V...  2.24 us

profile of v4, /device:TPU:1, one launch (start us, length us, event | category | flops | bytes accessed | tf_op | source)
XLA Modules:
  0.0 62.2 jit_solution(12771352493829286814)
XLA Ops:
  0.6 59.3 %attention.1 = (bf16[128,512]{1,0:T(8,128)(2,1)}, bf16[128,768]{1,0:T(8,128)(2,1)}, bf16[640,128]{1,0:T(8,128)(2,1)}, bf16[2,512,512]{2,1,0:T(8,128)(2,1)}) custom-call(bf16[128,768]{1,0:T(8,128)(2,1)} %refs_0_.1, bf16[576,128]{1,0:T(8,128)(2,1)} %bitcast.3, bf16[512,512]{1,0:T(8,128)(2,1)} %refs_2_.1, bf16[512,512]{1,0:T(8,128)(2,1)} %refs_3_.1, ...), custom_call_target="tpu_custom_call" | custom-call | tf_op jit(solution)/shard_map/attention/pallas_call | solution.py:646
  59.9 2.2 %write_out.1 = (bf16[128,512]{1,0:T(8,128)(2,1)}, bf16[128,768]{1,0:T(8,128)(2,1)}, bf16[576,128]{1,0:T(8,128)(2,1)}, bf16[512,512]{1,0:T(8,128)(2,1)}, bf16[512,512]{1,0:T(8,128)(2,1)}) custom-call(bf16[128,512]{1,0:T(8,128)(2,1)} %get-tuple-element.14.attn, bf16[128,768]{1,0:T(8,128)(2,1)} %get-tuple-element.15.gq, bf16[640,128]{1,0:T(8,128)(2,1)} %get-tuple-element.16.gl, ...), custom_call_target="tpu_custom_call" | custom-call | tf_op jit(solution)/shard_map/write_out/pallas_call | solution.py:715

commit v5 on v4

v5 whole, which is shorter than its diff:
```python
import functools
import math

import jax
import jax.numpy as jnp
from jax import lax
from jax.experimental import pallas as pl
from jax.experimental.pallas import tpu as pltpu
from jax.sharding import PartitionSpec as P

LAT = 512
ROPE = 64
NOPE = 128
VDIM = 128
PREV = 4
NZ = 8
NY = 4
TOK = 128
WIN = (PREV + 1) * TOK
QK = NOPE + ROPE
HEADS = 4
PIECES = (((0, 1), 256), ((2, 3), 256))
WIDE = [len(heads) * NOPE for heads, _ in PIECES]
FIRST = [heads[0] * NOPE for heads, _ in PIECES]
A_ROWS = [a_rows for _, a_rows in PIECES]
B_ROWS = [512 - a_rows for a_rows in A_ROWS]
FAR_Z = (4, 3, 5, 2, 6, 1, 7)
FAR_Y = (2, 1, 3)
MESH = pl.DeviceIdType.MESH
BF = jnp.bfloat16
SCALE = 1.0 / math.sqrt(QK)


def f32(x):
    return x.astype(jnp.float32)


def nn(a, b):
    return jnp.dot(a, b, preferred_element_type=jnp.float32)


def nt(a, b):
    return lax.dot_general(a, b, (((1,), (1,)), ((), ())), preferred_element_type=jnp.float32)


def mult(x, m):
    return pl.multiple_of(x, m)


def slot_cols(slot):
    return pl.ds(slot * TOK, TOK)


def kernel(n_ctx, n_head, *refs):
    (
        q_hbm,
        lat_hbm,
        wk_hbm,
        wv_hbm,
        do_hbm,
        seg_hbm,
        attn_out,
        gq_out,
        gl_out,
        gw_out,
        attn_ref,
        gq_ref,
        gl_ref,
        gw_ref,
        q_ref,
        wcat,
        do_ref,
        seg_ref,
        win,
        wt,
        qs,
        qt,
        dot,
        kt,
        vt,
        bias,
        raw_scores,
        raw_grads,
        dcat,
        rope_sum,
        *by_piece,
        glb,
        x_in,
        x_part,
        yl_in,
        ctx_part,
        ctx_in,
        load_sem,
        halo_s,
        halo_r,
        far_s,
        far_r,
        mate_s,
        mate_r,
        pair_s,
        pair_r,
        z_s,
        z_r,
        y_s,
        y_r,
        zy_s,
        zy_r,
        yz_s,
        yz_r,
        yzg_s,
        yzg_r,
        zg_s,
        zg_r,
        yg_s,
        yg_r,
        pairg_s,
        pairg_r,
        x_s,
        x_r,
        yl_s,
        yl_r,
        ctx_s,
        ctx_r,
        headg_s,
        headg_r,
        store_sem,
    ) = refs
    part, pair_in, half, z_in, zy_all, y_in, yz_in, y_part = (
        by_piece[i * len(PIECES) : (i + 1) * len(PIECES)] for i in range(8)
    )
    me = lax.axis_index("ctx")
    head = lax.axis_index("head")
    core = lax.rem(me, 2)
    z = lax.rem(me // 2, NZ)
    y = me // (2 * NZ)
    partner = me + 1 - 2 * core
    rows = glb.shape[0] // n_head
    x = head // 2
    y_lo = lax.rem(head, 2)
    head_rows = pl.ds(mult(head * rows, 16), rows)

    def z_dev(s):
        return {"ctx": (y * NZ + lax.rem(z + s, NZ)) * 2 + core}

    def y_dev(s):
        return {"ctx": (lax.rem(y + s, NY) * NZ + z) * 2 + core}

    def at_head(s):
        return lax.rem(head + s, n_head)

    def remote(src, dst, send, recv, device):
        return pltpu.make_async_remote_copy(
            src_ref=src, dst_ref=dst, send_sem=send, recv_sem=recv, device_id=device, device_id_type=MESH
        )

    def phase(block, send, recv):
        return remote(block, block, send, recv, {"ctx": partner})

    own_block = win.at[:, slot_cols(PREV)]
    loads = [
        pltpu.make_async_copy(src, dst, load_sem.at[i])
        for i, (src, dst) in enumerate(
            [(lat_hbm, own_block), (seg_hbm, seg_ref), (q_hbm, q_ref), (do_hbm, do_ref)]
            + [
                (
                    w.at[:, pl.ds(FIRST[p], WIDE[p])],
                    wcat.at[:, pl.ds(2 * FIRST[p] + kind * WIDE[p], WIDE[p])],
                )
                for p in range(len(PIECES))
                for kind, w in enumerate((wk_hbm, wv_hbm))
            ]
        )
    ]
    for load in loads:
        load.start()

    barrier = pltpu.get_barrier_semaphore()

    def greet(device):
        pl.semaphore_signal(barrier, inc=1, device_id=device, device_id_type=MESH)

    for s in (4, 2, 1, 3):

        @pl.when(me >= s)
        def _():
            greet({"ctx": me - s})

    for s in range(1, n_head):
        greet({"head": at_head(s)})
    greet({"ctx": partner})
    for s in range(1, n_head // 2):
        greet({"ctx": partner, "head": lax.rem(x + s, n_head // 2) * 2 + y_lo})
    for s in range(1, PREV + 1):

        @pl.when(me + s < n_ctx)
        def _():
            greet({"ctx": me + s})

    for s in range(1, NZ):
        greet(z_dev(s))
    for s in range(1, NY):
        greet(y_dev(s))

    pl.semaphore_wait(
        barrier,
        NZ - 1 + NY - 1 + n_head + n_head // 2 - 1 + jnp.minimum(me, PREV) + jnp.minimum(n_ctx - 1 - me, PREV),
    )

    x_peers = n_head // 2
    x_size = (LAT + ROPE) // x_peers
    x_rows = pl.ds(mult(x * x_size, 16), x_size)

    def x_dev(s):
        return {"head": lax.rem(x + s, x_peers) * 2 + y_lo}

    near = remote(lat_hbm, win.at[:, slot_cols(2)], halo_s.at[0], halo_r.at[0], {"ctx": me + 2})
    far = remote(
        lat_hbm.at[x_rows], win.at[x_rows, slot_cols(0)], halo_s.at[1], halo_r.at[1], {"ctx": me + 4}
    )

    def far_copy(s):
        block = win.at[x_rows, slot_cols(0)]
        return remote(block, block, far_s, far_r, x_dev(s))

    def cross_copy(s):
        return remote(
            win.at[x_rows, slot_cols(0)],
            win.at[x_rows, slot_cols(1)],
            mate_s.at[1],
            mate_r.at[1],
            {"ctx": partner} | x_dev(s),
        )

    def mate_copy(i, src):
        return remote(
            lat_hbm if src == PREV else win.at[:, slot_cols(src)],
            win.at[:, slot_cols(PREV - 1 - 2 * i)],
            mate_s.at[i],
            mate_r.at[i],
            {"ctx": partner},
        )

    @pl.when(me + 4 < n_ctx)
    def _():
        far.start()

    @pl.when(me + 2 < n_ctx)
    def _():
        near.start()

    @pl.when(core == 0)
    def _():
        mate_copy(0, PREV).start()

    far_all = phase(win.at[pl.ds(0, (x_peers - 1) * x_size), slot_cols(0)], far_s, far_r)

    for load in loads:
        load.wait()
    for h in range(HEADS):
        block = q_ref[:, pl.ds(h * QK, QK)]
        qs[h] = block
        qt[h] = block.T
        dot[h] = do_ref[:, pl.ds(h * VDIM, VDIM)].T
    own = seg_ref[pl.ds(me, 1), :]
    query_seg = jnp.broadcast_to(own, (TOK, TOK)).T
    for s in range(PREV + 1):
        place = me - PREV + s
        key_seg = jnp.where(place >= 0, seg_ref[pl.ds(jnp.maximum(place, 0), 1), :], -1)
        allowed = query_seg == key_seg
        if s == PREV:
            allowed &= lax.broadcasted_iota(jnp.int32, (TOK, TOK), 1) <= lax.broadcasted_iota(
                jnp.int32, (TOK, TOK), 0
            )
        bias[:, slot_cols(s)] = jnp.where(allowed, 0.0, -jnp.inf)

    @pl.when(me >= 4)
    def _():
        far.wait_recv()
        for s in FAR_Y:
            far_copy(s).start()

        @pl.when(core == 1)
        def _():
            for s in (*FAR_Y, 0):
                cross_copy(s).start()

    for i in range(4):
        wt[pl.ds(i * 256, 256), :] = wcat[:, pl.ds(i * 256, 256)].T
    def project(start, size):
        cols = pl.ds(start, size)
        for p, (heads, _) in enumerate(PIECES):
            first, wide = FIRST[p], WIDE[p]
            made = nn(wt[pl.ds(2 * first, 2 * wide), :], win[pl.ds(0, LAT), cols]).astype(BF)
            for j, h in enumerate(heads):
                kt[h, pl.ds(0, NOPE), cols] = made[j * NOPE : (j + 1) * NOPE]
                vt[h, :, cols] = made[wide + j * VDIM : wide + (j + 1) * VDIM]
        for h in range(HEADS):
            kt[h, pl.ds(NOPE, ROPE), cols] = win[pl.ds(LAT, ROPE), cols]

    def products(start, size):
        cols = pl.ds(start, size)
        for h in range(HEADS):
            raw_scores[h, :, cols] = nn(qs[h], kt[h, :, cols]) * SCALE + bias[:, cols]
            raw_grads[h, :, cols] = nn(do_ref[:, pl.ds(h * VDIM, VDIM)], vt[h, :, cols])

    project(PREV * TOK, TOK)

    @pl.when(me >= 2)
    def _():
        near.wait_recv()

    @pl.when(me < 2)
    def _():
        win[:, slot_cols(2)] = jnp.zeros((LAT + ROPE, TOK), BF)

    @pl.when(core == 0)
    def _():
        mate_copy(1, 2).start()

    @pl.when(core == 1)
    def _():
        mate_copy(0, 2).start()

    mate_copy(0, PREV).wait_recv()
    project(2 * TOK, 2 * TOK)
    products(2 * TOK, 3 * TOK)

    @pl.when(me >= 4)
    def _():
        far_all.wait_recv()

    @pl.when(me < 4)
    def _():
        win[:, slot_cols(0)] = jnp.zeros((LAT + ROPE, TOK), BF)

    @pl.when(me + 4 < n_ctx)
    def _():
        far.wait_send()

    @pl.when(me + 2 < n_ctx)
    def _():
        near.wait_send()

    @pl.when((core == 1) | (me >= 4))
    def _():
        mate_copy(1, PREV).wait_recv()

    @pl.when((core == 0) & (me < 4))
    def _():
        win[:, slot_cols(1)] = jnp.zeros((LAT + ROPE, TOK), BF)

    project(0, 2 * TOK)
    products(0, 2 * TOK)

    mate_copy(0, PREV).wait_send()

    @pl.when((core == 0) | (me >= 4))
    def _():
        mate_copy(1, PREV).wait_send()

    @pl.when(me >= 4)
    def _():
        far_all.wait_send()

    def some_heads(*heads):
        scores = [raw_scores[h] for h in heads]
        expo = [jnp.exp(a - jnp.max(a, axis=1, keepdims=True)) for a in scores]
        scaling = [1.0 / jnp.sum(a, axis=1, keepdims=True) for a in expo]
        out = [(nt(a.astype(BF), vt[h]) * b).astype(BF) for h, a, b in zip(heads, expo, scaling)]
        probs = [a * b for a, b in zip(expo, scaling)]
        for h, a in zip(heads, out):
            attn_ref[:, pl.ds(h * VDIM, VDIM)] = a
        delta = [
            jnp.sum(f32(do_ref[:, pl.ds(h * VDIM, VDIM)]) * f32(a), axis=1, keepdims=True)
            for h, a in zip(heads, out)
        ]
        grad_scores = [
            (a * (raw_grads[h] - b)).astype(BF) for h, a, b in zip(heads, probs, delta)
        ]
        for h, a, b in zip(heads, probs, grad_scores):
            p = [h in group for group, _ in PIECES].index(True)
            base = 2 * FIRST[p] + PIECES[p][0].index(h) * NOPE
            term = (nn(qt[h], b) * SCALE).astype(BF)
            dcat[pl.ds(base, NOPE), :] = term[:NOPE]
            rope_sum[...] = f32(term[NOPE:]) if h == 0 else rope_sum[...] + f32(term[NOPE:])
            dcat[pl.ds(base + WIDE[p], VDIM), :] = nn(dot[h], a.astype(BF)).astype(BF)
        for h, b in zip(heads, grad_scores):
            gq_ref[:, pl.ds(h * QK, QK)] = (nt(b, kt[h]) * SCALE).astype(BF)

    def pair_copy(p):
        return remote(
            part[p].at[1 - core], pair_in[p], pair_s.at[p], pair_r.at[p], {"ctx": partner}
        )

    def weight_terms(p):
        first, wide = FIRST[p], WIDE[p]
        terms = nt(win[pl.ds(0, LAT), :], dcat[pl.ds(2 * first, 2 * wide), :]).astype(BF)
        part[p][0] = terms[:, :wide]
        part[p][1] = terms[:, wide:]
        pair_copy(p).start()

    def z_rows(p, i):
        size = A_ROWS[p] // NZ
        return pl.ds(mult(i * size, size), size)

    def y_rows(p, i):
        size = B_ROWS[p] // NY
        return pl.ds(mult(A_ROWS[p] + i * size, size), size)

    def piece_cols(p):
        return pl.ds(FIRST[p], WIDE[p])

    def small(p, i):
        return pl.ds(mult(i // 2 * 16, 16), 16), pl.ds(mult(lax.rem(i, 2) * (WIDE[p] // 2), 128), WIDE[p] // 2)

    def z_copy(p, s):
        return remote(
            half[p].at[z_rows(p, lax.rem(z + s, NZ))], z_in[p].at[s - 1], z_s.at[p], z_r.at[p], z_dev(s)
        )

    def y_copy(p, s):
        return remote(
            half[p].at[y_rows(p, lax.rem(y + s, NY))], y_in[p].at[s - 1], y_s.at[p], y_r.at[p], y_dev(s)
        )

    def zy_copy(p, s):
        return remote(zy_all[p].at[y], zy_all[p].at[y], zy_s.at[p], zy_r.at[p], y_dev(s))

    def yz_copy(p, s):
        r, c = small(p, lax.rem(z + s, NZ))
        return remote(y_part[p].at[r, c], yz_in[p].at[s - 1], yz_s.at[p], yz_r.at[p], z_dev(s))

    def z_place(p):
        return gw_ref.at[z_rows(p, z), piece_cols(p)]

    def y_place(p):
        return gw_ref.at[y_rows(p, y), piece_cols(p)]

    def yz_place(p):
        size = B_ROWS[p] // NY
        r = pl.ds(mult(A_ROWS[p] + y * size + z // 2 * 16, 16), 16)
        return gw_ref.at[r, pl.ds(mult(FIRST[p] + lax.rem(z, 2) * (WIDE[p] // 2), 128), WIDE[p] // 2)]

    def yzg_copy(p, s):
        return remote(yz_place(p), yz_place(p), yzg_s.at[p], yzg_r.at[p], z_dev(s))

    def zg_copy(p, s):
        return remote(z_place(p), z_place(p), zg_s.at[p], zg_r.at[p], z_dev(s))

    def yg_copy(p, s):
        return remote(y_place(p), y_place(p), yg_s.at[p], yg_r.at[p], y_dev(s))

    def pairg_copy(p):
        return remote(
            gw_ref.at[:, piece_cols(p)],
            gw_out.at[core, :, piece_cols(p)],
            pairg_s.at[p],
            pairg_r.at[p],
            {"ctx": partner},
        )

    def keep_copy(p):
        return pltpu.make_async_copy(
            gw_ref.at[:, piece_cols(p)], gw_out.at[core, :, piece_cols(p)], store_sem.at[p]
        )

    def z_phase(p):
        return phase(z_in[p], z_s.at[p], z_r.at[p])

    def y_phase(p):
        return phase(y_in[p], y_s.at[p], y_r.at[p])

    def zy_phase(p):
        return phase(zy_all[p].at[pl.ds(0, NY - 1)], zy_s.at[p], zy_r.at[p])

    def yz_phase(p):
        return phase(yz_in[p], yz_s.at[p], yz_r.at[p])

    def yzg_phase(p):
        return phase(yz_in[p], yzg_s.at[p], yzg_r.at[p])

    def zg_phase(p):
        return phase(z_in[p], zg_s.at[p], zg_r.at[p])

    def yg_phase(p):
        return phase(y_in[p], yg_s.at[p], yg_r.at[p])

    def stage_a(p):
        pair_copy(p).wait_recv()
        a, b = pl.ds(0, A_ROWS[p]), pl.ds(A_ROWS[p], B_ROWS[p])
        if B_ROWS[p]:
            half[p][b, :] = (f32(part[p][core, b, :]) + f32(pair_in[p][b, :])).astype(BF)
            for s in FAR_Y:
                y_copy(p, s).start()
        half[p][a, :] = (f32(part[p][core, a, :]) + f32(pair_in[p][a, :])).astype(BF)
        for s in FAR_Z:
            z_copy(p, s).start()
        pair_copy(p).wait_send()

    def stage_b(p):
        if B_ROWS[p]:
            y_phase(p).wait_recv()
            total = f32(half[p][y_rows(p, y), :])
            for s in range(1, NY):
                total += f32(y_in[p][s - 1])
            y_part[p][...] = total.astype(BF)
            for s in FAR_Z:
                yz_copy(p, s).start()
        z_phase(p).wait_recv()
        total = f32(half[p][z_rows(p, z), :])
        for s in range(1, NZ):
            total += f32(z_in[p][s - 1])
        zy_all[p][y] = total.astype(BF)
        for s in FAR_Y:
            zy_copy(p, s).start()
        z_phase(p).wait_send()
        if B_ROWS[p]:
            y_phase(p).wait_send()

    def stage_c(p):
        if B_ROWS[p]:
            yz_phase(p).wait_recv()
            r, c = small(p, z)
            total = f32(y_part[p][r, c])
            for s in range(1, NZ):
                total += f32(yz_in[p][s - 1])
            yz_place(p)[...] = total.astype(BF)
            for s in FAR_Z:
                yzg_copy(p, s).start()
        zy_phase(p).wait_recv()
        total = f32(zy_all[p][0])
        for i in range(1, NY):
            total += f32(zy_all[p][i])
        z_place(p)[...] = total.astype(BF)
        for s in FAR_Z:
            zg_copy(p, s).start()
        zy_phase(p).wait_send()
        if B_ROWS[p]:
            yz_phase(p).wait_send()

    def stage_d(p):
        yzg_phase(p).wait_recv()
        for s in FAR_Y:
            yg_copy(p, s).start()
        yzg_phase(p).wait_send()

    def stage_e(p):
        zg_phase(p).wait_recv()
        if B_ROWS[p]:
            yg_phase(p).wait_recv()
        pairg_copy(p).start()
        keep_copy(p).start()
        zg_phase(p).wait_send()
        if B_ROWS[p]:
            yg_phase(p).wait_send()

    def x_copy(s):
        there = lax.rem(x + s, x_peers)
        return remote(
            glb.at[pl.ds(mult(there * 2 * rows, 16), 2 * rows)],
            x_in.at[s - 1],
            x_s,
            x_r,
            x_dev(s),
        )

    def yl_copy():
        return remote(
            x_part.at[pl.ds(mult((1 - y_lo) * rows, 16), rows)],
            yl_in,
            yl_s,
            yl_r,
            {"head": head + 1 - 2 * y_lo},
        )

    def ctx_copy(s):
        return remote(
            ctx_part.at[:, slot_cols(PREV - s)],
            ctx_in.at[s - 1],
            ctx_s.at[s - 1],
            ctx_r.at[s - 1],
            {"ctx": me - s},
        )

    def headg_copy(s):
        return remote(
            gl_ref.at[head_rows], gl_out.at[head_rows], headg_s, headg_r, {"head": at_head(s)}
        )

    def own_rows():
        return pltpu.make_async_copy(gl_ref.at[head_rows], gl_out.at[head_rows], store_sem.at[len(PIECES)])

    def head_outputs():
        return [
            pltpu.make_async_copy(attn_ref, attn_out, store_sem.at[len(PIECES) + 1]),
            pltpu.make_async_copy(gq_ref, gq_out, store_sem.at[len(PIECES) + 2]),
        ]

    def latent_terms():
        glb[pl.ds(0, LAT), :] = nn(wcat[...], dcat[...]).astype(BF)
        glb[pl.ds(LAT, ROPE), :] = rope_sum[...].astype(BF)
        glb[pl.ds(LAT + ROPE, glb.shape[0] - LAT - ROPE), :] = jnp.zeros(
            (glb.shape[0] - LAT - ROPE, WIN), BF
        )
        for s in FAR_Y:
            x_copy(s).start()

    def latent_x():
        phase(x_in, x_s, x_r).wait_recv()
        total = f32(glb[pl.ds(mult(x * 2 * rows, 16), 2 * rows), :])
        for s in range(1, x_peers):
            total += f32(x_in[s - 1])
        x_part[...] = total.astype(BF)
        yl_copy().start()
        phase(x_in, x_s, x_r).wait_send()

    def latent_y():
        yl_copy().wait_recv()
        total = f32(x_part[pl.ds(mult(y_lo * rows, 16), rows), :]) + f32(yl_in[...])
        ctx_part[...] = total.astype(BF)
        for s in range(1, PREV + 1):

            @pl.when(me >= s)
            def _():
                ctx_copy(s).start()

        yl_copy().wait_send()

    def latent_blocks():
        for s in range(1, PREV + 1):

            @pl.when(me + s < n_ctx)
            def _():
                ctx_copy(s).wait_recv()

            @pl.when(me + s >= n_ctx)
            def _():
                ctx_in[s - 1] = jnp.zeros(ctx_in.shape[1:], BF)

        total = f32(ctx_part[:, slot_cols(PREV)])
        for s in range(1, PREV + 1):
            total += f32(ctx_in[s - 1])
        gl_ref[head_rows, :] = total.astype(BF)
        for s in FAR_Z:
            headg_copy(s).start()
        own_rows().start()

    some_heads(0, 1)
    weight_terms(0)
    some_heads(2, 3)
    stage_a(0)
    weight_terms(1)
    latent_terms()
    for copy in head_outputs():
        copy.start()
    stage_a(1)
    stage_b(0)
    stage_b(1)
    stage_c(0)
    stage_c(1)
    latent_x()
    stage_d(0)
    stage_d(1)
    latent_y()
    stage_e(0)
    latent_blocks()
    stage_e(1)

    for s in range(1, PREV + 1):

        @pl.when(me >= s)
        def _():
            ctx_copy(s).wait_send()

    phase(gl_out.at[pl.ds(0, (n_head - 1) * rows)], headg_s, headg_r).wait()
    own_rows().wait()
    for copy in head_outputs():
        copy.wait()
    for p in range(len(PIECES)):
        pairg_copy(p).wait()
        keep_copy(p).wait()


def write_out(attn, gq, gl, gw, attn_out, gq_out, gl_out, gk_out, gv_out, *rest):
    stages, load_sem, store_sem = rest[:5], rest[5], rest[6]
    parts = [(gw.at[k, pl.ds(i * 128, 128)], out.at[pl.ds(i * 128, 128)]) for k, out in ((0, gk_out), (1, gv_out)) for i in range(4)]
    parts += [(gq, gq_out), (gl.at[pl.ds(0, LAT + ROPE)], gl_out), (attn, attn_out)]
    spots = [stages[0].at[pl.ds(i * 128, 128)] for i in range(4)]
    spots += [stages[1].at[pl.ds(i * 128, 128)] for i in range(4)]
    spots += list(stages[2:])
    loads = [
        pltpu.make_async_copy(src, spot, load_sem.at[i])
        for i, ((src, _), spot) in enumerate(zip(parts, spots))
    ]
    stores = [
        pltpu.make_async_copy(spot, dst, store_sem.at[i])
        for i, ((_, dst), spot) in enumerate(zip(parts, spots))
    ]
    for load in loads:
        load.start()
    for load, store in zip(loads, stores):
        load.wait()
        store.start()
    for store in stores:
        store.wait()


def per_device(queries, latent, w_key, w_value, grad_out, segment_ids):
    n_ctx = lax.axis_size("ctx")
    n_head = lax.axis_size("head")
    hbm = pl.BlockSpec(memory_space=pltpu.HBM)
    dma = pltpu.SemaphoreType.DMA
    rows = 80

    def buf(*shape, dtype=BF):
        return pltpu.VMEM(shape, dtype)

    def sems(*shape):
        return [dma(shape), dma(shape)]

    attn_out, grad_queries, grad_latent, grad_w = pl.pallas_call(
        functools.partial(kernel, n_ctx, n_head),
        out_shape=[
            jax.ShapeDtypeStruct((TOK, HEADS * VDIM), BF),
            jax.ShapeDtypeStruct((TOK, HEADS * QK), BF),
            jax.ShapeDtypeStruct((rows * n_head, TOK), BF),
            jax.ShapeDtypeStruct((2, LAT, HEADS * NOPE), BF),
        ],
        in_specs=[hbm] * 6,
        out_specs=[hbm] * 4,
        scratch_shapes=[
            buf(TOK, HEADS * VDIM),
            buf(TOK, HEADS * QK),
            buf(rows * n_head, TOK),
            buf(LAT, HEADS * NOPE),
            buf(TOK, HEADS * QK),
            buf(LAT, 2 * HEADS * NOPE),
            buf(TOK, HEADS * VDIM),
            buf(n_ctx, TOK, dtype=jnp.int32),
            buf(LAT + ROPE, WIN),
            buf(2 * HEADS * NOPE, LAT),
            buf(HEADS, TOK, QK),
            buf(HEADS, QK, TOK),
            buf(HEADS, VDIM, TOK),
            buf(HEADS, QK, WIN),
            buf(HEADS, VDIM, WIN),
            buf(TOK, WIN, dtype=jnp.float32),
            buf(HEADS, TOK, WIN, dtype=jnp.float32),
            buf(HEADS, TOK, WIN, dtype=jnp.float32),
            buf(2 * HEADS * NOPE, WIN),
            buf(ROPE, WIN, dtype=jnp.float32),
            *[buf(2, LAT, wide) for wide in WIDE],
            *[buf(LAT, wide) for wide in WIDE],
            *[buf(LAT, wide) for wide in WIDE],
            *[buf(NZ - 1, a // NZ, wide) for a, wide in zip(A_ROWS, WIDE)],
            *[buf(NY, a // NZ, wide) for a, wide in zip(A_ROWS, WIDE)],
            *[buf(NY - 1, max(b // NY, 16), wide) for b, wide in zip(B_ROWS, WIDE)],
            *[buf(NZ - 1, 16, max(wide // 2, 128)) for wide in WIDE],
            *[buf(max(b // NY, 16), wide) for b, wide in zip(B_ROWS, WIDE)],
            buf(rows * n_head, WIN),
            buf(n_head // 2 - 1, 2 * rows, WIN),
            buf(2 * rows, WIN),
            buf(rows, WIN),
            buf(rows, WIN),
            buf(PREV, rows, TOK),
            dma((4 + 2 * len(PIECES),)),
            *sems(2),
            dma,
            dma,
            *sems(2),
            *sems(len(PIECES)),
            *sems(len(PIECES)),
            *sems(len(PIECES)),
            *sems(len(PIECES)),
            *sems(len(PIECES)),
            *sems(len(PIECES)),
            *sems(len(PIECES)),
            *sems(len(PIECES)),
            *sems(len(PIECES)),
            dma,
            dma,
            dma,
            dma,
            *sems(PREV),
            dma,
            dma,
            dma((len(PIECES) + 3,)),
        ],
        compiler_params=pltpu.CompilerParams(
            collective_id=0, has_side_effects=True, vmem_limit_bytes=60 * 2**20
        ),
        name="attention",
    )(queries, latent.T, w_key, w_value, grad_out, segment_ids.reshape(n_ctx, TOK))
    any_space = pl.BlockSpec(memory_space=pl.ANY)
    attn_out, grad_queries, grad_latent, grad_w_key, grad_w_value = pl.pallas_call(
        write_out,
        out_shape=[
            jax.ShapeDtypeStruct((TOK, HEADS * VDIM), BF),
            jax.ShapeDtypeStruct((TOK, HEADS * QK), BF),
            jax.ShapeDtypeStruct((LAT + ROPE, TOK), BF),
            jax.ShapeDtypeStruct((LAT, HEADS * NOPE), BF),
            jax.ShapeDtypeStruct((LAT, HEADS * NOPE), BF),
        ],
        in_specs=[any_space] * 4,
        out_specs=[hbm] * 5,
        scratch_shapes=[
            buf(LAT, HEADS * NOPE),
            buf(LAT, HEADS * NOPE),
            buf(TOK, HEADS * QK),
            buf(LAT + ROPE, TOK),
            buf(TOK, HEADS * VDIM),
            *sems(11),
        ],
        compiler_params=pltpu.CompilerParams(vmem_limit_bytes=60 * 2**20),
        name="write_out",
    )(attn_out, grad_queries, grad_latent, grad_w)
    return (attn_out, grad_queries, grad_latent.T, grad_w_key, grad_w_value)


def solution(mesh):
    return jax.shard_map(
        per_device,
        mesh=mesh,
        in_specs=(
            P("ctx", "head"),
            P("ctx", None),
            P(None, "head"),
            P(None, "head"),
            P("ctx", "head"),
            P(),
        ),
        out_specs=(
            P("ctx", "head"),
            P("ctx", "head"),
            P("ctx", None),
            P(None, "head"),
            P(None, "head"),
        ),
        check_vma=False,
    )
```

time: 63 us -> 61.9 us (0.983); the launches traced: 62.2 us -> 61.8 us
  no operation moved by 1% of the time
where the time goes in v5:
time: 61.9 us; the launch traced here: 61.8 us
  Pallas kernels  61.1 us (99%)
  between operations  0.64 us (1%)
    pallas_call x1, Pallas kernels, per_device(): pl.pallas_call(functools.partial(kernel, n_ctx, n_head), out_shape=[jax.S...  58.8 us
    pallas_call x1, Pallas kernels, per_device(): pl.pallas_call(write_out, out_shape=[jax.ShapeDtypeStruct((TOK, HEADS * V...  2.31 us

profile of v5, /device:TPU:1, one launch (start us, length us, event | category | flops | bytes accessed | tf_op | source)
XLA Modules:
  0.0 61.8 jit_solution(11627595650527964720)
XLA Ops:
  0.6 58.8 %attention.1 = (bf16[128,512]{1,0:T(8,128)(2,1)}, bf16[128,768]{1,0:T(8,128)(2,1)}, bf16[640,128]{1,0:T(8,128)(2,1)}, bf16[2,512,512]{2,1,0:T(8,128)(2,1)}) custom-call(bf16[128,768]{1,0:T(8,128)(2,1)} %refs_0_.1, bf16[576,128]{1,0:T(8,128)(2,1)} %bitcast.3, bf16[512,512]{1,0:T(8,128)(2,1)} %refs_2_.1, bf16[512,512]{1,0:T(8,128)(2,1)} %refs_3_.1, ...), custom_call_target="tpu_custom_call" | custom-call | tf_op jit(solution)/shard_map/attention/pallas_call | solution.py:721
  59.5 2.3 %write_out.1 = (bf16[128,512]{1,0:T(8,128)(2,1)}, bf16[128,768]{1,0:T(8,128)(2,1)}, bf16[576,128]{1,0:T(8,128)(2,1)}, bf16[512,512]{1,0:T(8,128)(2,1)}, bf16[512,512]{1,0:T(8,128)(2,1)}) custom-call(bf16[128,512]{1,0:T(8,128)(2,1)} %get-tuple-element.14.attn, bf16[128,768]{1,0:T(8,128)(2,1)} %get-tuple-element.15.gq, bf16[640,128]{1,0:T(8,128)(2,1)} %get-tuple-element.16.gl, ...), custom_call_target="tpu_custom_call" | custom-call | tf_op jit(solution)/shard_map/write_out/pallas_call | solution.py:795

commit v6 on v5

--- a/solution.py
+++ b/solution.py
@@ -554,11 +554,14 @@
         if B_ROWS[p]:
             yg_phase(p).wait_send()
 
-    def x_copy(s):
+    x_full = 2 * rows
+    x_last = LAT + ROPE - (x_peers - 1) * x_full
+
+    def x_copy(s, size):
         there = lax.rem(x + s, x_peers)
         return remote(
-            glb.at[pl.ds(mult(there * 2 * rows, 16), 2 * rows)],
-            x_in.at[s - 1],
+            glb.at[pl.ds(mult(there * x_full, 16), size)],
+            x_in.at[s - 1, pl.ds(0, size)],
             x_s,
             x_r,
             x_dev(s),
@@ -603,16 +606,42 @@
             (glb.shape[0] - LAT - ROPE, WIN), BF
         )
         for s in FAR_Y:
-            x_copy(s).start()
+
+            @pl.when(lax.rem(x + s, x_peers) < x_peers - 1)
+            def _():
+                x_copy(s, x_full).start()
+
+            @pl.when(lax.rem(x + s, x_peers) == x_peers - 1)
+            def _():
+                x_copy(s, x_last).start()
+
 
     def latent_x():
-        phase(x_in, x_s, x_r).wait_recv()
+        @pl.when(x < x_peers - 1)
+        def _():
+            phase(x_in, x_s, x_r).wait_recv()
+
+        @pl.when(x == x_peers - 1)
+        def _():
+            x_in[:, pl.ds(x_last, x_full - x_last), :] = jnp.zeros(
+                (x_peers - 1, x_full - x_last, WIN), BF
+            )
+            phase(x_in.at[:, pl.ds(0, x_last)], x_s, x_r).wait_recv()
+
         total = f32(glb[pl.ds(mult(x * 2 * rows, 16), 2 * rows), :])
         for s in range(1, x_peers):
             total += f32(x_in[s - 1])
         x_part[...] = total.astype(BF)
         yl_copy().start()
-        phase(x_in, x_s, x_r).wait_send()
+
+        @pl.when(x < x_peers - 1)
+        def _():
+            sent = (x_peers - 2) * x_full + x_last
+            phase(glb.at[pl.ds(0, sent)], x_s, x_r).wait_send()
+
+        @pl.when(x == x_peers - 1)
+        def _():
+            phase(x_in, x_s, x_r).wait_send()
 
     def latent_y():
         yl_copy().wait_recv()

time: 61.9 us -> 62.2 us (level)
  no operation moved by 1% of the time
where the time goes in v6:
time: 62.2 us; the launch traced here: 62 us
  Pallas kernels  61.4 us (99%)
  between operations  0.64 us (1%)
    pallas_call x1, Pallas kernels, per_device(): pl.pallas_call(functools.partial(kernel, n_ctx, n_head), out_shape=[jax.S...  59.1 us
    pallas_call x1, Pallas kernels, per_device(): pl.pallas_call(write_out, out_shape=[jax.ShapeDtypeStruct((TOK, HEADS * V...  2.31 us

profile of v6, /device:TPU:1, one launch (start us, length us, event | category | flops | bytes accessed | tf_op | source)
XLA Modules:
  0.0 62.0 jit_solution(13112874497165443663)
XLA Ops:
  0.6 59.1 %attention.1 = (bf16[128,512]{1,0:T(8,128)(2,1)}, bf16[128,768]{1,0:T(8,128)(2,1)}, bf16[640,128]{1,0:T(8,128)(2,1)}, bf16[2,512,512]{2,1,0:T(8,128)(2,1)}) custom-call(bf16[128,768]{1,0:T(8,128)(2,1)} %refs_0_.1, bf16[576,128]{1,0:T(8,128)(2,1)} %bitcast.3, bf16[512,512]{1,0:T(8,128)(2,1)} %refs_2_.1, bf16[512,512]{1,0:T(8,128)(2,1)} %refs_3_.1, ...), custom_call_target="tpu_custom_call" | custom-call | tf_op jit(solution)/shard_map/attention/pallas_call | solution.py:750
  59.7 2.3 %write_out.1 = (bf16[128,512]{1,0:T(8,128)(2,1)}, bf16[128,768]{1,0:T(8,128)(2,1)}, bf16[576,128]{1,0:T(8,128)(2,1)}, bf16[512,512]{1,0:T(8,128)(2,1)}, bf16[512,512]{1,0:T(8,128)(2,1)}) custom-call(bf16[128,512]{1,0:T(8,128)(2,1)} %get-tuple-element.14.attn, bf16[128,768]{1,0:T(8,128)(2,1)} %get-tuple-element.15.gq, bf16[640,128]{1,0:T(8,128)(2,1)} %get-tuple-element.16.gl, ...), custom_call_target="tpu_custom_call" | custom-call | tf_op jit(solution)/shard_map/write_out/pallas_call | solution.py:824
